TPU v7x, 32 devices: a whole 2x2x4 slice. The times are simulated.
32 devices in a mesh: pipe: 4 (over y, x), dp: 8 (over z, core).
Axes of the slice: x: 2, y: 2, z: 4, core: 2. Of those that a mesh axis runs over, the one named last changes fastest.
Arguments:
- inputs: bfloat16 [4, 64, 8192], P('pipe', 'dp'), may hold values from -6 to 6
- cotangent: bfloat16 [4, 64, 8192], P('pipe', 'dp'), may hold values from -6 to 6
- norm_gain: float32 [4, 8192], P('pipe'), may hold values from 0.1 to 1.9
- w_value: bfloat16 [4, 64, 8192], P('pipe'), may hold values from -0.0625 to 0.0625
- w_out: bfloat16 [4, 64, 8192], P('pipe'), may hold values from -0.75 to 0.75
- value_down: bfloat16 [4, 8, 16, 8192], P('pipe', 'dp'), may hold values from -0.0625 to 0.0625
- value_up_factor: bfloat16 [4, 8, 16, 64], P('pipe', 'dp'), may hold values from -1.5 to 1.5
- out_down: bfloat16 [4, 8, 16, 64], P('pipe', 'dp'), may hold values from -0.75 to 0.75
- output_up_factor: bfloat16 [4, 8, 16, 8192], P('pipe', 'dp'), may hold values from -1.5 to 1.5
- block_tenant: int32 [8], replicated, may hold values from 0 to 7
- valid_tokens: int32 [8], replicated, may hold values from 1 to 32, 192 in all
- tenant_slot: int32 [8], replicated, may hold values from 0 to 7, each once
Outputs:
- grad_value_down: bfloat16 [4, 8, 16, 8192], P('pipe', 'dp')
- grad_value_up: bfloat16 [4, 8, 16, 64], P('pipe', 'dp')
- grad_out_down: bfloat16 [4, 8, 16, 64], P('pipe', 'dp')
- grad_out_up: bfloat16 [4, 8, 16, 8192], P('pipe', 'dp')
Inputs may be any that keep to these rules, and one draw needn't show every extreme that they name: `block_tenant`: tenant whose adapters serve all 32 tokens of a dp index. The first valid_tokens[i] block positions of dp index i are valid, the rest padding. A permutation: the adapters and gradients of tenant t sit at slot tenant_slot[t], stored on dp index tenant_slot[t].
All inputs are finite; a program needn't handle non-finite values.
Results may differ from a plain program's by a relative error of at most 0.034.
Values may be sent and summed in bfloat16 or wider, within the bound.
A program may use at most 64 MiB of HBM per device.

v0:
```python
import jax
import jax.numpy as jnp
from jax import lax
from jax.sharding import PartitionSpec as P

adapter_scale = 2.0
norm_eps = 1e-05


def from_behind(value, axis, by):
    peers = lax.axis_size(axis)
    return lax.ppermute(value, axis, [(i, (i + by) % peers) for i in range(peers)])


def normalize(token_rows, gain_row):
    wide_rows = token_rows.astype(jnp.float32)
    inverse = lax.rsqrt(jnp.mean(wide_rows * wide_rows, axis=-1, keepdims=True) + norm_eps)
    return ((wide_rows * inverse * gain_row).astype(jnp.bfloat16), inverse)


def contract_trailing(left, right):
    return lax.dot_general(
        left, right, (((1,), (1,)), ((), ())), preferred_element_type=jnp.float32
    )


def contract_leading(left, right):
    return lax.dot_general(
        left, right, (((0,), (0,)), ((), ())), preferred_element_type=jnp.float32
    )


def section_parts(token_rows, gain_row, value_weight, tenant_adapters):
    value_down, value_up_factor, out_down, output_up_factor = tenant_adapters
    normalized_rows, inverse = normalize(token_rows, gain_row)
    lowrank_product = contract_trailing(normalized_rows, value_down).astype(jnp.bfloat16)
    value_blend = contract_trailing(normalized_rows, value_weight)
    value_blend = value_blend + adapter_scale * jnp.dot(
        lowrank_product, value_up_factor, preferred_element_type=jnp.float32
    )
    value_row_block = value_blend.astype(jnp.bfloat16)
    sidepath_rank = contract_trailing(value_row_block, out_down).astype(jnp.bfloat16)
    return (normalized_rows, inverse, lowrank_product, value_row_block, sidepath_rank)


def section_output(token_rows, layer_pieces, out_weight, tenant_adapters):
    blended_rows = token_rows.astype(jnp.float32) + jnp.dot(
        layer_pieces[3], out_weight, preferred_element_type=jnp.float32
    )
    blended_rows = blended_rows + adapter_scale * jnp.dot(
        layer_pieces[4], tenant_adapters[3], preferred_element_type=jnp.float32
    )
    return blended_rows.astype(jnp.bfloat16)


def section_backward(
    token_rows, input_gradient, layer_pieces, gain_row, value_weight, out_weight, tenant_adapters
):
    value_down, value_up_factor, out_down, output_up_factor = tenant_adapters
    normalized_rows, inverse, lowrank_product, value_row_block, sidepath_rank = layer_pieces
    sidepath_gradient = (
        adapter_scale * contract_trailing(input_gradient, output_up_factor)
    ).astype(jnp.bfloat16)
    value_gradient = contract_trailing(input_gradient, out_weight)
    value_gradient = (
        value_gradient + jnp.dot(sidepath_gradient, out_down, preferred_element_type=jnp.float32)
    ).astype(jnp.bfloat16)
    lowrank_gradient = (adapter_scale * contract_trailing(value_gradient, value_up_factor)).astype(
        jnp.bfloat16
    )
    grad_normed = jnp.dot(
        value_gradient, value_weight, preferred_element_type=jnp.float32
    ) + jnp.dot(lowrank_gradient, value_down, preferred_element_type=jnp.float32)
    scaled = grad_normed * gain_row
    wide_rows = token_rows.astype(jnp.float32)
    correction = jnp.mean(scaled * wide_rows, axis=-1, keepdims=True)
    grad_rows = inverse * scaled - wide_rows * (inverse * inverse * inverse) * correction
    grad_out = (input_gradient.astype(jnp.float32) + grad_rows).astype(jnp.bfloat16)
    gradient_pieces = (
        contract_leading(lowrank_gradient, normalized_rows),
        adapter_scale * contract_leading(lowrank_product, value_gradient),
        contract_leading(sidepath_gradient, value_row_block),
        adapter_scale * contract_leading(sidepath_rank, input_gradient),
    )
    return (grad_out, gradient_pieces)


def pass_section(token_rows, shift_by):
    return from_behind(token_rows, "pipe", shift_by)


def owner_layout(first, second, third, fourth):
    return (
        lax.all_to_all(first, "dp", split_axis=0, concat_axis=2, tiled=True),
        lax.all_to_all(second, "dp", split_axis=0, concat_axis=2, tiled=True),
        lax.all_to_all(third, "dp", split_axis=0, concat_axis=2, tiled=True),
        lax.all_to_all(fourth, "dp", split_axis=0, concat_axis=2, tiled=True),
    )


def pick_rows(picker, sliced_part):
    flat_rows = sliced_part.reshape(sliced_part.shape[0], -1)
    chosen = jnp.dot(picker, flat_rows, preferred_element_type=jnp.float32).astype(jnp.bfloat16)
    return chosen.reshape((picker.shape[0],) + sliced_part.shape[1:])


def sum_by_slot(slot_float, gathered_part):
    flat_rows = gathered_part.reshape(gathered_part.shape[0], -1)
    summed = lax.dot_general(
        slot_float,
        flat_rows,
        (((0,), (0,)), ((), ())),
        precision=lax.Precision.HIGHEST,
        preferred_element_type=jnp.float32,
    )
    return summed.astype(jnp.bfloat16).reshape((slot_float.shape[1],) + gathered_part.shape[1:])


def put_entry(stash, entry, micro_index, active):

    def update(stored_all, new_entry):
        previous = lax.dynamic_index_in_dim(stored_all, micro_index, 0, keepdims=False)
        return lax.dynamic_update_index_in_dim(
            stored_all, jnp.where(active, new_entry, previous), micro_index, 0
        )

    return jax.tree.map(update, stash, entry)


def get_entry(stash, micro_index):
    return jax.tree.map(
        lambda stored_all: lax.dynamic_index_in_dim(stored_all, micro_index, 0, keepdims=False),
        stash,
    )


def body(
    inputs,
    cotangent,
    norm_gain,
    w_value,
    w_out,
    value_down,
    value_up_factor,
    out_down,
    output_up_factor,
    block_tenant,
    valid_tokens,
    tenant_slot,
):
    section_index = lax.axis_index("pipe")
    sections = lax.axis_size("pipe")
    member = lax.axis_index("dp")
    members = lax.axis_size("dp")
    queue_depth = inputs.shape[0]
    row_count = inputs.shape[1]
    micro_count = queue_depth * sections
    ticks = micro_count + sections - 1
    tenant_ids = jnp.arange(tenant_slot.shape[0], dtype=jnp.int32)
    tenant_hot = block_tenant[:, None] == tenant_ids[None, :]
    slot_of = jnp.sum(jnp.where(tenant_hot, tenant_slot[None, :], 0), axis=1)
    slot_hot = slot_of[:, None] == tenant_ids[None, :]
    member_hot = jnp.arange(members, dtype=jnp.int32) == member
    own_tenant = jnp.sum(jnp.where(member_hot, block_tenant, 0))
    own_valid = jnp.sum(jnp.where(member_hot, valid_tokens, 0))
    tenant_tokens = jnp.sum(jnp.where(block_tenant == own_tenant, valid_tokens, 0)).astype(
        jnp.float32
    )
    sliced = (
        lax.all_to_all(value_down[0], "dp", split_axis=2, concat_axis=0, tiled=True),
        lax.all_to_all(value_up_factor[0], "dp", split_axis=2, concat_axis=0, tiled=True),
        lax.all_to_all(out_down[0], "dp", split_axis=2, concat_axis=0, tiled=True),
        lax.all_to_all(output_up_factor[0], "dp", split_axis=2, concat_axis=0, tiled=True),
    )
    picker = slot_hot.astype(jnp.bfloat16)
    picked = [pick_rows(picker, sliced_part) for sliced_part in sliced]
    fetched = owner_layout(picked[0], picked[1], picked[2], picked[3])
    tenant_adapters = tuple((whole_part[0] for whole_part in fetched))
    gain_row = norm_gain[0]
    value_weight = w_value[0]
    out_weight = w_out[0]

    def token_weight(micro_index):
        position = micro_index * row_count + jnp.arange(row_count, dtype=jnp.int32)
        return (
            jnp.where(position < own_valid, 1.0, 0.0).astype(jnp.float32)[:, None] / tenant_tokens
        )

    def keep_entry(current):
        return (current,)

    def parts_of(entry):
        return section_parts(entry[0], gain_row, value_weight, tenant_adapters)

    blank = jnp.zeros((row_count, inputs.shape[2]), jnp.bfloat16)
    sample = keep_entry(blank)
    stash = jax.tree.map(
        lambda leaf_value: jnp.zeros((micro_count,) + leaf_value.shape, leaf_value.dtype), sample
    )
    accum = tuple((jnp.zeros(adapter_part.shape, jnp.float32) for adapter_part in tenant_adapters))

    def forward_tick(tick_index, arriving, feed_rows, stash_now, order):
        position = tick_index - section_index
        active = (position >= 0) & (position < micro_count)
        micro_index = order(jnp.clip(position, 0, micro_count - 1))
        current = jnp.where(section_index == 0, feed_rows, arriving)
        layer_pieces = section_parts(current, gain_row, value_weight, tenant_adapters)
        result = section_output(current, layer_pieces, out_weight, tenant_adapters)
        stash_now = put_entry(stash_now, keep_entry(current), micro_index, active)
        return (result, stash_now)

    def backward_tick(tick_index, arriving, feed_rows, stash_now, accum_now, order):
        position = tick_index - (sections - 1 - section_index)
        active = (position >= 0) & (position < micro_count)
        micro_index = order(jnp.clip(position, 0, micro_count - 1))
        entry = get_entry(stash_now, micro_index)
        seeded = (feed_rows.astype(jnp.float32) * token_weight(micro_index)).astype(jnp.bfloat16)
        input_gradient = jnp.where(section_index == sections - 1, seeded, arriving)
        grad_out, gradient_pieces = section_backward(
            entry[0],
            input_gradient,
            parts_of(entry),
            gain_row,
            value_weight,
            out_weight,
            tenant_adapters,
        )
        accum_now = tuple(
            (
                running + jnp.where(active, addend, 0.0)
                for running, addend in zip(accum_now, gradient_pieces)
            )
        )
        return (grad_out, accum_now)

    all_inputs, all_cotangents = (
        lax.all_gather(inputs, "pipe", axis=0, tiled=True),
        lax.all_gather(cotangent, "pipe", axis=0, tiled=True),
    )

    def plain_order(position):
        return position

    def forward_step(tick_index, carry):
        arriving, stash_now = carry
        feed_rows = lax.dynamic_index_in_dim(
            all_inputs, jnp.minimum(tick_index, micro_count - 1), 0, keepdims=False
        )
        result, stash_now = forward_tick(tick_index, arriving, feed_rows, stash_now, plain_order)
        return (pass_section(result, 1), stash_now)

    arriving, stash = lax.fori_loop(0, ticks, forward_step, (blank, stash))

    def backward_step(tick_index, carry):
        arriving, accum_now = carry
        feed_rows = lax.dynamic_index_in_dim(
            all_cotangents, jnp.minimum(tick_index, micro_count - 1), 0, keepdims=False
        )
        grad_out, accum_now = backward_tick(
            tick_index, arriving, feed_rows, stash, accum_now, plain_order
        )
        return (pass_section(grad_out, sections - 1), accum_now)

    arriving, accum = lax.fori_loop(0, ticks, backward_step, (blank, accum))
    spread = (
        lax.all_to_all(
            accum[0][None].astype(jnp.bfloat16), "dp", split_axis=2, concat_axis=0, tiled=True
        ).astype(jnp.float32),
        lax.all_to_all(
            accum[1][None].astype(jnp.bfloat16), "dp", split_axis=2, concat_axis=0, tiled=True
        ).astype(jnp.float32),
        lax.all_to_all(
            accum[2][None].astype(jnp.bfloat16), "dp", split_axis=2, concat_axis=0, tiled=True
        ).astype(jnp.float32),
        lax.all_to_all(
            accum[3][None].astype(jnp.bfloat16), "dp", split_axis=2, concat_axis=0, tiled=True
        ).astype(jnp.float32),
    )
    slot_float = slot_hot.astype(jnp.float32)
    totals = [sum_by_slot(slot_float, gathered_part) for gathered_part in spread]
    owned = owner_layout(totals[0], totals[1], totals[2], totals[3])
    return (owned[0][None], owned[1][None], owned[2][None], owned[3][None])


def solution(mesh):
    return jax.shard_map(
        body,
        mesh=mesh,
        in_specs=(
            P("pipe", "dp", None),
            P("pipe", "dp", None),
            P("pipe", None),
            P("pipe", None, None),
            P("pipe", None, None),
            P("pipe", "dp", None, None),
            P("pipe", "dp", None, None),
            P("pipe", "dp", None, None),
            P("pipe", "dp", None, None),
            P(),
            P(),
            P(),
        ),
        out_specs=(
            P("pipe", "dp", None, None),
            P("pipe", "dp", None, None),
            P("pipe", "dp", None, None),
            P("pipe", "dp", None, None),
        ),
        check_vma=False,
    )
```

profile of v0, /device:TPU:0, one launch (start us, length us, event | category | flops | bytes accessed | tf_op | source)
XLA Modules:
  0.0 570.7 jit_solution(18041291288463908201)
XLA Ops:
  2.0 6.3 %all-to-all-start.2 = ((bf16[1,16,64]{1,0,2:T(2,128)(2,1)}), bf16[1,16,64]{1,0,2:T(2,128)(2,1)S(1)}, u32[]{:S(2)}, u32[]{:S(2)}) async-start(bf16[1,16,64]{1,0,2:T(2,128)(2,1)} %copy.102), calls=%async_computation.2 | async-start | bytes 65536 | tf_op jit(solution)/shard_map/all_to_all | solution.py:171
  35.4 8.3 %copy.98 = bf16[1,16,8192]{1,0,2:T(2,128)(2,1)} copy(bf16[1,16,8192]{2,1,0:T(8,128)(2,1)} %bitcast.321) | data formatting | bytes 524288 | tf_op jit(solution)/shard_map/squeeze | solution.py:170
  44.3 45.2 %reduce = bf16[8192,16]{1,0:T(8,128)(2,1)S(1)} reduce(bf16[8192,1,16]{2,1,0:T(2,128)(2,1)} %bitcast.297, bf16[]{:T(256)} %broadcast.230), dimensions={1}, to_apply=%bitcast.150.reduce_sub_computation | reduce | bytes 524290
  92.3 5.2 all-to-all-start
  97.6 6.7 %copy.108 = bf16[1,16,8192]{1,0,2:T(2,128)(2,1)} copy(bf16[1,16,8192]{2,1,0:T(8,128)(2,1)S(1)} %bitcast.322) | data formatting | bytes 524288 | tf_op jit(solution)/shard_map/squeeze | solution.py:173
  104.3 45.2 %reduce.1 = bf16[8192,16]{1,0:T(8,128)(2,1)S(1)} reduce(bf16[8192,1,16]{2,1,0:T(2,128)(2,1)} %bitcast.304, bf16[]{:T(256)} %broadcast.230), dimensions={1}, to_apply=%bitcast.152.reduce_sub_computation | reduce | bytes 524290
  152.3 5.1 all-to-all-start.6
  157.4 5.1 reshape.150
  162.5 7.9 %copy.99 = bf16[1,16,8192]{2,1,0:T(8,128)(2,1)S(1)} copy(bf16[1,16,8192]{1,0,2:T(2,128)(2,1)} %bitcast.299) | data formatting | bytes 524288 | tf_op jit(solution)/shard_map/all_to_all | solution.py:170
  176.8 5.1 reshape.152
  181.9 8.0 %copy.109 = bf16[1,16,8192]{2,1,0:T(8,128)(2,1)S(1)} copy(bf16[1,16,8192]{1,0,2:T(2,128)(2,1)} %bitcast.300) | data formatting | bytes 524288 | tf_op jit(solution)/shard_map/all_to_all | solution.py:173
  198.9 11.9 %all_gather.7 = bf16[4,8,8192]{2,1,0:T(8,128)(2,1)} all-gather(bf16[1,8,8192]{2,1,0:T(8,128)(2,1)S(1)} %copy-done.4), channel_id=1, replica_groups=mesh['pipe'=4,'dp'=8] {'pipe'}, dimensions={0}, use_global_device_ids=true | all-gather | bytes 655360 | tf_op jit(solution)/shard_map/all_gather | solution.py:237
  210.8 10.3 %all_gather.6 = bf16[4,8,8192]{2,1,0:T(8,128)(2,1)} all-gather(bf16[1,8,8192]{2,1,0:T(8,128)(2,1)S(1)} %copy-done.5), channel_id=1, replica_groups=mesh['pipe'=4,'dp'=8] {'pipe'}, dimensions={0}, use_global_device_ids=true | all-gather | bytes 655360 | tf_op jit(solution)/shard_map/all_gather | solution.py:238
  221.5 72.6 %while.40 = (s32[]{:T(128)}, bf16[8,8192]{1,0:T(8,128)(2,1)S(1)}, bf16[4,8,8192]{2,1,0:T(8,128)(2,1)S(1)}, pred[]{:T(512)}, bf16[4,8,8192]{2,1,0:T(8,128)(2,1)},...) while((s32[]{:T(128)}, bf16[8,8192]{1,0:T(8,128)(2,1)S(1)}, ...), condition=%wide.region_3.4_spmd, body=%wide.region_1.3_spmd.sunk | while | flops 22185748 | bytes 5320154 | solution.py:252
  236.1 5.7 collective-permute-done
  246.0 5.8 %collective-permute-done = bf16[8,8192]{1,0:T(8,128)(2,1)S(1)} collective-permute-done((bf16[8,8192]{1,0:T(8,128)(2,1)S(1)}, bf16[8,8192]{1,0:T(8,128)(2,1)S(1)}, u32[]{:S(2)}, u32[]{:S(2)}) %collective-permute-start) | collective-permute-done | bytes 131104 | tf_op jit(solution)/shard_map/while/body/eval_jaxpr/ppermute | solution.py:12
  256.2 5.8 %collective-permute-done = bf16[8,8192]{1,0:T(8,128)(2,1)S(1)} collective-permute-done((bf16[8,8192]{1,0:T(8,128)(2,1)S(1)}, bf16[8,8192]{1,0:T(8,128)(2,1)S(1)}, u32[]{:S(2)}, u32[]{:S(2)}) %collective-permute-start) | collective-permute-done | bytes 131104 | tf_op jit(solution)/shard_map/while/body/eval_jaxpr/ppermute | solution.py:12
  266.3 6.5 %collective-permute-done = bf16[8,8192]{1,0:T(8,128)(2,1)S(1)} collective-permute-done((bf16[8,8192]{1,0:T(8,128)(2,1)S(1)}, bf16[8,8192]{1,0:T(8,128)(2,1)S(1)}, u32[]{:S(2)}, u32[]{:S(2)}) %collective-permute-start) | collective-permute-done | bytes 131104 | tf_op jit(solution)/shard_map/while/body/eval_jaxpr/ppermute | solution.py:12
  277.1 6.8 %collective-permute-done = bf16[8,8192]{1,0:T(8,128)(2,1)S(1)} collective-permute-done((bf16[8,8192]{1,0:T(8,128)(2,1)S(1)}, bf16[8,8192]{1,0:T(8,128)(2,1)S(1)}, u32[]{:S(2)}, u32[]{:S(2)}) %collective-permute-start) | collective-permute-done | bytes 131104 | tf_op jit(solution)/shard_map/while/body/eval_jaxpr/ppermute | solution.py:12
  288.2 5.8 %collective-permute-done = bf16[8,8192]{1,0:T(8,128)(2,1)S(1)} collective-permute-done((bf16[8,8192]{1,0:T(8,128)(2,1)S(1)}, bf16[8,8192]{1,0:T(8,128)(2,1)S(1)}, u32[]{:S(2)}, u32[]{:S(2)}) %collective-permute-start) | collective-permute-done | bytes 131104 | tf_op jit(solution)/shard_map/while/body/eval_jaxpr/ppermute | solution.py:12
  294.1 73.1 %while.41 = (s32[]{:T(128)}, bf16[8,8192]{1,0:T(8,128)(2,1)S(1)}, f32[16,8192]{1,0:T(8,128)}, f32[16,64]{1,0:T(8,128)S(1)}, f32[16,64]{1,0:T(8,128)S(1)}, /*inde...) while((s32[]{:T(128)}, bf16[8,8192]{1,0:T(8,128)(2,1)S(1)}, ...), condition=%wide.region_10.11_spmd.clone, body=%wide.region_7.10_spmd.clone.sunk | while | flops 38709568 | bytes 9483558 | solution.py:264
  400.8 6.7 %copy.126 = bf16[1,16,8192]{1,0,2:T(2,128)(2,1)} copy(bf16[1,16,8192]{2,1,0:T(8,128)(2,1)S(1)} %get-tuple-element.948) | data formatting | bytes 524288 | tf_op jit(solution)/shard_map/convert_element_type | solution.py:276
  407.5 45.2 %reduce.3 = bf16[8192,16]{1,0:T(8,128)(2,1)S(1)} reduce(bf16[8192,1,16]{2,1,0:T(2,128)(2,1)} %bitcast.301, bf16[]{:T(256)} %broadcast.230), dimensions={1}, to_apply=%bitcast.156.reduce_sub_computation | reduce | bytes 524290
  455.5 5.3 all-to-all-start.14
  460.8 6.7 %copy.116 = bf16[1,16,8192]{1,0,2:T(2,128)(2,1)} copy(bf16[1,16,8192]{2,1,0:T(8,128)(2,1)S(1)} %get-tuple-element.949) | data formatting | bytes 524288 | tf_op jit(solution)/shard_map/convert_element_type | solution.py:267
  467.5 45.2 %reduce.2 = bf16[8192,16]{1,0:T(8,128)(2,1)S(1)} reduce(bf16[8192,1,16]{2,1,0:T(2,128)(2,1)} %bitcast.298, bf16[]{:T(256)} %broadcast.230), dimensions={1}, to_apply=%bitcast.154.reduce_sub_computation | reduce | bytes 524290
  515.6 5.1 all-to-all-start.8
  520.7 5.1 reshape.156
  525.8 7.9 %copy.127 = bf16[1,16,8192]{2,1,0:T(8,128)(2,1)S(1)} copy(bf16[1,16,8192]{1,0,2:T(2,128)(2,1)} %bitcast.302) | data formatting | bytes 524288 | tf_op jit(solution)/shard_map/all_to_all | solution.py:275
  540.1 5.1 reshape.154
  545.2 7.9 %copy.117 = bf16[1,16,8192]{2,1,0:T(8,128)(2,1)S(1)} copy(bf16[1,16,8192]{1,0,2:T(2,128)(2,1)} %bitcast.303) | data formatting | bytes 524288 | tf_op jit(solution)/shard_map/all_to_all | solution.py:266
  561.8 7.4 %all-to-all-done.9 = bf16[8,16,1024]{2,1,0:T(8,128)(2,1)S(1)} async-done(((bf16[8,16,1024]{2,1,0:T(8,128)(2,1)}), bf16[8,16,1024]{2,1,0:T(8,128)(2,1)S(1)}, u32[]{:S(2)}, u32[]{:S(2)}) %all-to-all-start.9) | async-done | bytes 262176 | tf_op jit(solution)/shard_map/all_to_all | solution.py:94
  (307 shorter events, 213.7 us)
Async XLA Ops:
  2.0 12.1 %all-to-all-start.2 = ((bf16[1,16,64]{1,0,2:T(2,128)(2,1)}), bf16[1,16,64]{1,0,2:T(2,128)(2,1)S(1)}, u32[]{:S(2)}, u32[]{:S(2)}) async-start(bf16[1,16,64]{1,0,2:T(2,128)(2,1)} %copy.102), calls=%async_computation.2 | async-start | bytes 65536 | tf_op jit(solution)/shard_map/all_to_all | solution.py:171
  14.1 9.0 %all-to-all-start.4 = ((bf16[1,16,64]{1,0,2:T(2,128)(2,1)}), bf16[1,16,64]{1,0,2:T(2,128)(2,1)S(1)}, u32[]{:S(2)}, u32[]{:S(2)}) async-start(bf16[1,16,64]{1,0,2:T(2,128)(2,1)} %copy.105), calls=%async_computation.4 | async-start | bytes 65536 | tf_op jit(solution)/shard_map/all_to_all | solution.py:172
  23.1 8.9 %all-to-all-start.3 = ((bf16[8,16,8]{1,2,0:T(8,128)(2,1)}), bf16[8,16,8]{1,2,0:T(8,128)(2,1)S(1)}, u32[]{:S(2)}, u32[]{:S(2)}) async-start(bf16[8,16,8]{1,2,0:T(8,128)(2,1)} %copy.104), calls=%async_computation.3 | async-start | bytes 32768 | tf_op jit(solution)/shard_map/all_to_all | solution.py:95
  32.0 60.3 %all-to-all-start.5 = ((bf16[8,16,8]{1,2,0:T(8,128)(2,1)}), bf16[8,16,8]{1,2,0:T(8,128)(2,1)S(1)}, u32[]{:S(2)}, u32[]{:S(2)}) async-start(bf16[8,16,8]{1,2,0:T(8,128)(2,1)} %copy.107), calls=%async_computation.5 | async-start | bytes 32768 | tf_op jit(solution)/shard_map/all_to_all | solution.py:96
  44.2 53.3 %copy-start.3 = (bf16[1,1,16,8192]{3,2,1,0:T(8,128)(2,1)S(1)}, bf16[1,1,16,8192]{3,2,1,0:T(8,128)(2,1)}, u32[]{:S(2)}) copy-start(bf16[1,1,16,8192]{3,2,1,0:T(8,128)(2,1)} %param.24) | copy-start | bytes 786436
  92.3 60.0 %all-to-all-start = ((bf16[8,2,8192]{2,1,0:T(2,128)(2,1)}), bf16[8,2,8192]{2,1,0:T(2,128)(2,1)S(1)}, u32[]{:S(2)}, u32[]{:S(2)}) async-start(bf16[8,2,8192]{2,1,0:T(2,128)(2,1)} %reshape.149), calls=%async_computation | async-start | bytes 524288 | tf_op jit(solution)/shard_map/all_to_all | solution.py:170
  152.3 19.4 %all-to-all-start.6 = ((bf16[8,2,8192]{2,1,0:T(2,128)(2,1)}), bf16[8,2,8192]{2,1,0:T(2,128)(2,1)S(1)}, u32[]{:S(2)}, u32[]{:S(2)}) async-start(bf16[8,2,8192]{2,1,0:T(2,128)(2,1)} %reshape.151), calls=%async_computation.6 | async-start | bytes 524288 | tf_op jit(solution)/shard_map/all_to_all | solution.py:173
  171.7 19.6 %all-to-all-start.1 = ((bf16[8,16,1024]{2,1,0:T(8,128)(2,1)}), bf16[8,16,1024]{2,1,0:T(8,128)(2,1)S(1)}, u32[]{:S(2)}, u32[]{:S(2)}) async-start(bf16[8,16,1024]{2,1,0:T(8,128)(2,1)} %copy.100), calls=%async_computation.1 | async-start | bytes 524288 | tf_op jit(solution)/shard_map/all_to_all | solution.py:94
  181.9 39.5 %copy-start = (bf16[1,64,8192]{2,1,0:T(8,128)(2,1)S(1)}, bf16[1,64,8192]{2,1,0:T(8,128)(2,1)}, u32[]{:S(2)}) copy-start(bf16[1,64,8192]{2,1,0:T(8,128)(2,1)} %param.19) | copy-start | bytes 3145732
  191.2 30.1 %all-to-all-start.7 = ((bf16[8,16,1024]{2,1,0:T(8,128)(2,1)}), bf16[8,16,1024]{2,1,0:T(8,128)(2,1)S(1)}, u32[]{:S(2)}, u32[]{:S(2)}) async-start(bf16[8,16,1024]{2,1,0:T(8,128)(2,1)} %copy.110), calls=%async_computation.7 | async-start | bytes 524288 | tf_op jit(solution)/shard_map/all_to_all | solution.py:97
  225.7 5.9 %collective-permute-start = (bf16[8,8192]{1,0:T(8,128)(2,1)S(1)}, bf16[8,8192]{1,0:T(8,128)(2,1)S(1)}, u32[]{:S(2)}, u32[]{:S(2)}) collective-permute-start(bf16[8,8192]{1,0:T(8,128)(2,1)S(1)} %fusion.160), channel_id=1, source_target_pairs={{0,8},{8,16},{16,24},{24,0},{1,9},{9,17},{17,25},{25,1},{2,10},{10... | collective-permute-start | bytes 393224 | tf_op jit(solution)/shard_map/while/body/eval_jaxpr/ppermute | solution.py:12
  235.8 5.9 %collective-permute-start = (bf16[8,8192]{1,0:T(8,128)(2,1)S(1)}, bf16[8,8192]{1,0:T(8,128)(2,1)S(1)}, u32[]{:S(2)}, u32[]{:S(2)}) collective-permute-start(bf16[8,8192]{1,0:T(8,128)(2,1)S(1)} %fusion.160), channel_id=1, source_target_pairs={{0,8},{8,16},{16,24},{24,0},{1,9},{9,17},{17,25},{25,1},{2,10},{10... | collective-permute-start | bytes 393224 | tf_op jit(solution)/shard_map/while/body/eval_jaxpr/ppermute | solution.py:12
  246.0 5.9 %collective-permute-start = (bf16[8,8192]{1,0:T(8,128)(2,1)S(1)}, bf16[8,8192]{1,0:T(8,128)(2,1)S(1)}, u32[]{:S(2)}, u32[]{:S(2)}) collective-permute-start(bf16[8,8192]{1,0:T(8,128)(2,1)S(1)} %fusion.160), channel_id=1, source_target_pairs={{0,8},{8,16},{16,24},{24,0},{1,9},{9,17},{17,25},{25,1},{2,10},{10... | collective-permute-start | bytes 393224 | tf_op jit(solution)/shard_map/while/body/eval_jaxpr/ppermute | solution.py:12
  256.1 5.9 %collective-permute-start = (bf16[8,8192]{1,0:T(8,128)(2,1)S(1)}, bf16[8,8192]{1,0:T(8,128)(2,1)S(1)}, u32[]{:S(2)}, u32[]{:S(2)}) collective-permute-start(bf16[8,8192]{1,0:T(8,128)(2,1)S(1)} %fusion.160), channel_id=1, source_target_pairs={{0,8},{8,16},{16,24},{24,0},{1,9},{9,17},{17,25},{25,1},{2,10},{10... | collective-permute-start | bytes 393224 | tf_op jit(solution)/shard_map/while/body/eval_jaxpr/ppermute | solution.py:12
  266.2 6.6 %collective-permute-start = (bf16[8,8192]{1,0:T(8,128)(2,1)S(1)}, bf16[8,8192]{1,0:T(8,128)(2,1)S(1)}, u32[]{:S(2)}, u32[]{:S(2)}) collective-permute-start(bf16[8,8192]{1,0:T(8,128)(2,1)S(1)} %fusion.160), channel_id=1, source_target_pairs={{0,8},{8,16},{16,24},{24,0},{1,9},{9,17},{17,25},{25,1},{2,10},{10... | collective-permute-start | bytes 393224 | tf_op jit(solution)/shard_map/while/body/eval_jaxpr/ppermute | solution.py:12
  277.1 6.9 %collective-permute-start = (bf16[8,8192]{1,0:T(8,128)(2,1)S(1)}, bf16[8,8192]{1,0:T(8,128)(2,1)S(1)}, u32[]{:S(2)}, u32[]{:S(2)}) collective-permute-start(bf16[8,8192]{1,0:T(8,128)(2,1)S(1)} %fusion.160), channel_id=1, source_target_pairs={{0,8},{8,16},{16,24},{24,0},{1,9},{9,17},{17,25},{25,1},{2,10},{10... | collective-permute-start | bytes 393224 | tf_op jit(solution)/shard_map/while/body/eval_jaxpr/ppermute | solution.py:12
  288.2 5.9 %collective-permute-start = (bf16[8,8192]{1,0:T(8,128)(2,1)S(1)}, bf16[8,8192]{1,0:T(8,128)(2,1)S(1)}, u32[]{:S(2)}, u32[]{:S(2)}) collective-permute-start(bf16[8,8192]{1,0:T(8,128)(2,1)S(1)} %fusion.160), channel_id=1, source_target_pairs={{0,8},{8,16},{16,24},{24,0},{1,9},{9,17},{17,25},{25,1},{2,10},{10... | collective-permute-start | bytes 393224 | tf_op jit(solution)/shard_map/while/body/eval_jaxpr/ppermute | solution.py:12
  297.9 5.2 collective-permute-start.1
  306.9 6.5 %collective-permute-start.1 = (bf16[8,8192]{1,0:T(8,128)(2,1)}, bf16[8,8192]{1,0:T(8,128)(2,1)S(1)}, u32[]{:S(2)}, u32[]{:S(2)}) collective-permute-start(bf16[8,8192]{1,0:T(8,128)(2,1)} %fusion.196), channel_id=1, source_target_pairs={{0,24},{8,0},{16,8},{24,16},{1,25},{9,1},{17,9},{25,17},{2,26},{10... | collective-permute-start | bytes 393224 | tf_op jit(solution)/shard_map/while/body/eval_jaxpr/ppermute | solution.py:12
  317.3 7.3 %collective-permute-start.1 = (bf16[8,8192]{1,0:T(8,128)(2,1)}, bf16[8,8192]{1,0:T(8,128)(2,1)S(1)}, u32[]{:S(2)}, u32[]{:S(2)}) collective-permute-start(bf16[8,8192]{1,0:T(8,128)(2,1)} %fusion.196), channel_id=1, source_target_pairs={{0,24},{8,0},{16,8},{24,16},{1,25},{9,1},{17,9},{25,17},{2,26},{10... | collective-permute-start | bytes 393224 | tf_op jit(solution)/shard_map/while/body/eval_jaxpr/ppermute | solution.py:12
  328.4 6.5 %collective-permute-start.1 = (bf16[8,8192]{1,0:T(8,128)(2,1)}, bf16[8,8192]{1,0:T(8,128)(2,1)S(1)}, u32[]{:S(2)}, u32[]{:S(2)}) collective-permute-start(bf16[8,8192]{1,0:T(8,128)(2,1)} %fusion.196), channel_id=1, source_target_pairs={{0,24},{8,0},{16,8},{24,16},{1,25},{9,1},{17,9},{25,17},{2,26},{10... | collective-permute-start | bytes 393224 | tf_op jit(solution)/shard_map/while/body/eval_jaxpr/ppermute | solution.py:12
  338.7 7.1 %collective-permute-start.1 = (bf16[8,8192]{1,0:T(8,128)(2,1)}, bf16[8,8192]{1,0:T(8,128)(2,1)S(1)}, u32[]{:S(2)}, u32[]{:S(2)}) collective-permute-start(bf16[8,8192]{1,0:T(8,128)(2,1)} %fusion.196), channel_id=1, source_target_pairs={{0,24},{8,0},{16,8},{24,16},{1,25},{9,1},{17,9},{25,17},{2,26},{10... | collective-permute-start | bytes 393224 | tf_op jit(solution)/shard_map/while/body/eval_jaxpr/ppermute | solution.py:12
  349.6 6.5 %collective-permute-start.1 = (bf16[8,8192]{1,0:T(8,128)(2,1)}, bf16[8,8192]{1,0:T(8,128)(2,1)S(1)}, u32[]{:S(2)}, u32[]{:S(2)}) collective-permute-start(bf16[8,8192]{1,0:T(8,128)(2,1)} %fusion.196), channel_id=1, source_target_pairs={{0,24},{8,0},{16,8},{24,16},{1,25},{9,1},{17,9},{25,17},{2,26},{10... | collective-permute-start | bytes 393224 | tf_op jit(solution)/shard_map/while/body/eval_jaxpr/ppermute | solution.py:12
  360.0 7.3 %collective-permute-start.1 = (bf16[8,8192]{1,0:T(8,128)(2,1)}, bf16[8,8192]{1,0:T(8,128)(2,1)S(1)}, u32[]{:S(2)}, u32[]{:S(2)}) collective-permute-start(bf16[8,8192]{1,0:T(8,128)(2,1)} %fusion.196), channel_id=1, source_target_pairs={{0,24},{8,0},{16,8},{24,16},{1,25},{9,1},{17,9},{25,17},{2,26},{10... | collective-permute-start | bytes 393224 | tf_op jit(solution)/shard_map/while/body/eval_jaxpr/ppermute | solution.py:12
  367.9 10.3 %all-to-all-start.10 = ((bf16[1,16,64]{1,0,2:T(2,128)(2,1)}), bf16[1,16,64]{1,0,2:T(2,128)(2,1)S(1)}, u32[]{:S(2)}, u32[]{:S(2)}) async-start(bf16[1,16,64]{1,0,2:T(2,128)(2,1)} %copy.120), calls=%async_computation.10 | async-start | bytes 65536 | tf_op jit(solution)/shard_map/all_to_all | solution.py:269
  378.2 9.0 %all-to-all-start.12 = ((bf16[1,16,64]{1,0,2:T(2,128)(2,1)}), bf16[1,16,64]{1,0,2:T(2,128)(2,1)S(1)}, u32[]{:S(2)}, u32[]{:S(2)}) async-start(bf16[1,16,64]{1,0,2:T(2,128)(2,1)} %copy.123), calls=%async_computation.12 | async-start | bytes 65536 | tf_op jit(solution)/shard_map/all_to_all | solution.py:272
  387.2 8.9 %all-to-all-start.11 = ((bf16[8,16,8]{1,2,0:T(8,128)(2,1)}), bf16[8,16,8]{1,2,0:T(8,128)(2,1)S(1)}, u32[]{:S(2)}, u32[]{:S(2)}) async-start(bf16[8,16,8]{1,2,0:T(8,128)(2,1)} %copy.122), calls=%async_computation.11 | async-start | bytes 32768 | tf_op jit(solution)/shard_map/all_to_all | solution.py:95
  396.2 59.3 %all-to-all-start.13 = ((bf16[8,16,8]{1,2,0:T(8,128)(2,1)}), bf16[8,16,8]{1,2,0:T(8,128)(2,1)S(1)}, u32[]{:S(2)}, u32[]{:S(2)}) async-start(bf16[8,16,8]{1,2,0:T(8,128)(2,1)} %copy.125), calls=%async_computation.13 | async-start | bytes 32768 | tf_op jit(solution)/shard_map/all_to_all | solution.py:96
  455.5 60.1 %all-to-all-start.14 = ((bf16[8,2,8192]{2,1,0:T(2,128)(2,1)}), bf16[8,2,8192]{2,1,0:T(2,128)(2,1)S(1)}, u32[]{:S(2)}, u32[]{:S(2)}) async-start(bf16[8,2,8192]{2,1,0:T(2,128)(2,1)} %reshape.155), calls=%async_computation.14 | async-start | bytes 524288 | tf_op jit(solution)/shard_map/all_to_all | solution.py:275
  515.6 19.4 %all-to-all-start.8 = ((bf16[8,2,8192]{2,1,0:T(2,128)(2,1)}), bf16[8,2,8192]{2,1,0:T(2,128)(2,1)S(1)}, u32[]{:S(2)}, u32[]{:S(2)}) async-start(bf16[8,2,8192]{2,1,0:T(2,128)(2,1)} %reshape.153), calls=%async_computation.8 | async-start | bytes 524288 | tf_op jit(solution)/shard_map/all_to_all | solution.py:266
  535.0 19.4 %all-to-all-start.15 = ((bf16[8,16,1024]{2,1,0:T(8,128)(2,1)}), bf16[8,16,1024]{2,1,0:T(8,128)(2,1)S(1)}, u32[]{:S(2)}, u32[]{:S(2)}) async-start(bf16[8,16,1024]{2,1,0:T(8,128)(2,1)} %copy.128), calls=%async_computation.15 | async-start | bytes 524288 | tf_op jit(solution)/shard_map/all_to_all | solution.py:97
  554.4 14.8 %all-to-all-start.9 = ((bf16[8,16,1024]{2,1,0:T(8,128)(2,1)}), bf16[8,16,1024]{2,1,0:T(8,128)(2,1)S(1)}, u32[]{:S(2)}, u32[]{:S(2)}) async-start(bf16[8,16,1024]{2,1,0:T(8,128)(2,1)} %copy.118), calls=%async_computation.9 | async-start | bytes 524288 | tf_op jit(solution)/shard_map/all_to_all | solution.py:94
  (6 other events, 154.7 us)
where the time goes:
time: 581 us; the launch traced here: 571 us
  other arithmetic  210 us (36%)
  local copies, waits for them, and re-layouts  108 us (19%)
  starting transfers between devices  81.2 us (14%)
  waiting for transfers between devices  76.5 us (13%)
  matrix products  70.3 us (12%)
  blocking collectives  22.2 us (4%)
    unnamed x8, other arithmetic  181 us
    ppermute x14, waiting for transfers between devices, from_behind(): lax.ppermute(value, axis, [(i, (i + by) % peers) for i in range(peers)])  43 us
    unnamed x37, local copies, waits for them, and re-layouts  34.4 us
    dot_general x28, matrix products, contract_leading(): lax.dot_general(left, right, (((0,), (0,)), ((), ())), preferred_element_...  31.4 us
    dot_general x42, matrix products, contract_trailing(): lax.dot_general(left, right, (((1,), (1,)), ((), ())), preferred_element_...  12.8 us
    all_gather x1, blocking collectives, body(): lax.all_gather(inputs, 'pipe', axis=0, tiled=True)  11.9 us
  transfers between devices with their start and end apart: 30, of which 15 were waited for; matrix products, arithmetic and copies ran while one was open for 58% of the time, Pallas kernels for 0%

commit v1 on v0

--- a/solution.py
+++ b/solution.py
@@ -5,6 +5,7 @@
 
 adapter_scale = 2.0
 norm_eps = 1e-05
+stash_limit = 8 * 2**20
 
 
 def from_behind(value, axis, by):
@@ -134,7 +135,7 @@
     )
 
 
-def body(
+def relay_body(
     inputs,
     cotangent,
     norm_gain,
@@ -282,29 +283,168 @@
     return (owned[0][None], owned[1][None], owned[2][None], owned[3][None])
 
 
+def trail(left, right):
+    return lax.dot_general(
+        left, right, (((1,), (1,)), ((), ())), preferred_element_type=jnp.float32
+    )
+
+
+def plain(left, right):
+    return jnp.dot(left, right, preferred_element_type=jnp.float32)
+
+
+def row_weights(block_tenant, valid_tokens, tenant_slot, member, micro_count, row_count):
+    tenant_ids = jnp.arange(tenant_slot.shape[0], dtype=jnp.int32)
+    tenant_hot = block_tenant[:, None] == tenant_ids[None, :]
+    slot_of = jnp.sum(jnp.where(tenant_hot, tenant_slot[None, :], 0), axis=1)
+    same = block_tenant[:, None] == block_tenant[None, :]
+    tokens = jnp.sum(jnp.where(same, valid_tokens[None, :], 0), axis=1).astype(jnp.float32)
+    position = jnp.arange(micro_count * row_count, dtype=jnp.int32)
+    keep = (position[None, :] < valid_tokens[:, None]) & (slot_of[:, None] == member)
+    return jnp.where(keep, 1.0, 0.0).astype(jnp.float32) / tokens[:, None]
+
+
+def forward_small(projection, inverse, up_turned, out_down):
+    hd = projection.shape[0] - out_down.shape[0]
+    scaled = projection * inverse
+    lowrank = scaled[hd:].astype(jnp.bfloat16)
+    value = (scaled[:hd] + adapter_scale * plain(up_turned, lowrank)).astype(jnp.bfloat16)
+    side = plain(out_down, value).astype(jnp.bfloat16)
+    return lowrank, value, side
+
+
+def backward_small(back, up_factor, down_turned):
+    hd = up_factor.shape[1]
+    grad_side = (adapter_scale * back[hd:]).astype(jnp.bfloat16)
+    grad_value = (back[:hd] + plain(down_turned, grad_side)).astype(jnp.bfloat16)
+    grad_low = (adapter_scale * plain(up_factor, grad_value)).astype(jnp.bfloat16)
+    return grad_side, grad_value, grad_low
+
+
+def columns_body(
+    inputs,
+    cotangent,
+    norm_gain,
+    w_value,
+    w_out,
+    value_down,
+    value_up_factor,
+    out_down,
+    output_up_factor,
+    block_tenant,
+    valid_tokens,
+    tenant_slot,
+):
+    section = lax.axis_index("pipe")
+    sections = lax.axis_size("pipe")
+    member = lax.axis_index("dp")
+    row_count, width = inputs.shape[1:]
+    micro_count = inputs.shape[0] * sections
+    gain = norm_gain[0][None]
+    into = jnp.concatenate([w_value[0], value_down[0, 0]]).astype(jnp.float32) * gain
+    into = into.astype(jnp.bfloat16)
+    outof = jnp.concatenate([w_out[0], output_up_factor[0, 0]])
+    weights = lax.all_to_all(
+        jnp.stack([into, outof])[None], "pipe", split_axis=3, concat_axis=0, tiled=True
+    )
+    factors = lax.all_gather(
+        jnp.stack([value_up_factor[0, 0], out_down[0, 0]]), "pipe", axis=0
+    )
+    tokens = lax.all_to_all(
+        jnp.stack([inputs, cotangent], axis=1), "pipe", split_axis=3, concat_axis=0, tiled=True
+    )
+    tokens = lax.all_gather(tokens, "dp", axis=0)
+    columns = tokens.shape[-1]
+    rows = tokens[:, :, 0].reshape(-1, columns)
+    weight = row_weights(
+        block_tenant, valid_tokens, tenant_slot, member, micro_count, row_count
+    ).reshape(-1, 1)
+    gradient = (tokens[:, :, 1].reshape(-1, columns).astype(jnp.float32) * weight).astype(
+        jnp.bfloat16
+    )
+    kept = []
+    for layer in range(sections):
+        wide = rows.astype(jnp.float32)
+        squares = jnp.sum(wide * wide, axis=1)[None]
+        partial = jnp.concatenate([trail(weights[layer, 0], rows), squares])
+        whole = lax.psum(partial, "pipe")
+        projection = whole[:-1]
+        inverse = lax.rsqrt(whole[-1:] / width + norm_eps)
+        lowrank, value, side = forward_small(
+            projection, inverse, factors[layer, 0].T, factors[layer, 1]
+        )
+        kept.append((rows, projection, inverse, lowrank, value, side))
+        if layer < sections - 1:
+            mixed = jnp.concatenate([value, adapter_scale * side])
+            rows = (wide + contract_leading(mixed, weights[layer, 1])).astype(jnp.bfloat16)
+    downs, ups, small_ups, small_downs = [], [], [], []
+    for layer in reversed(range(sections)):
+        rows, projection, inverse, lowrank, value, side = kept[layer]
+        back = lax.psum(trail(weights[layer, 1], gradient), "pipe")
+        grad_side, grad_value, grad_low = backward_small(
+            back, factors[layer, 0], factors[layer, 1].T
+        )
+        both = jnp.concatenate([grad_value, grad_low]).astype(jnp.float32)
+        correction = jnp.sum(both * projection, axis=0, keepdims=True) / width
+        scaled = (both * inverse).astype(jnp.bfloat16)
+        downs.append(plain(scaled[value.shape[0] :], rows).astype(jnp.bfloat16))
+        ups.append((adapter_scale * plain(side, gradient)).astype(jnp.bfloat16))
+        small_ups.append((adapter_scale * trail(lowrank, grad_value)).astype(jnp.bfloat16))
+        small_downs.append(trail(grad_side, value).astype(jnp.bfloat16))
+        if layer > 0:
+            shrink = (inverse * inverse * inverse * correction).reshape(-1, 1)
+            gradient = (
+                gradient.astype(jnp.float32)
+                + contract_leading(scaled, weights[layer, 0])
+                - rows.astype(jnp.float32) * shrink
+            ).astype(jnp.bfloat16)
+    wide_pair = jnp.stack([jnp.stack(downs[::-1]), jnp.stack(ups[::-1])], axis=1)
+    wide_pair = lax.all_to_all(wide_pair, "pipe", split_axis=0, concat_axis=3, tiled=True)[0]
+    value_down_grad = (wide_pair[0].astype(jnp.float32) * gain).astype(jnp.bfloat16)
+    own_up = lax.dynamic_index_in_dim(jnp.stack(small_ups[::-1]), section, 0, keepdims=False)
+    own_down = lax.dynamic_index_in_dim(jnp.stack(small_downs[::-1]), section, 0, keepdims=False)
+    return (
+        value_down_grad[None, None],
+        own_up[None, None],
+        own_down[None, None],
+        wide_pair[1][None, None],
+    )
+
+
 def solution(mesh):
-    return jax.shard_map(
-        body,
-        mesh=mesh,
-        in_specs=(
-            P("pipe", "dp", None),
-            P("pipe", "dp", None),
-            P("pipe", None),
-            P("pipe", None, None),
-            P("pipe", None, None),
-            P("pipe", "dp", None, None),
-            P("pipe", "dp", None, None),
-            P("pipe", "dp", None, None),
-            P("pipe", "dp", None, None),
-            P(),
-            P(),
-            P(),
-        ),
-        out_specs=(
-            P("pipe", "dp", None, None),
-            P("pipe", "dp", None, None),
-            P("pipe", "dp", None, None),
-            P("pipe", "dp", None, None),
-        ),
-        check_vma=False,
-    )
+    sections = mesh.shape["pipe"]
+
+    def run(*arrays):
+        depth, row_total, width = arrays[0].shape
+        kept_bytes = 2 * depth * row_total * (width // sections) * sections
+        chosen = columns_body if kept_bytes <= stash_limit else relay_body
+        return place(chosen)(*arrays)
+
+    def place(chosen):
+        return jax.shard_map(
+            chosen,
+            mesh=mesh,
+            in_specs=(
+                P("pipe", "dp", None),
+                P("pipe", "dp", None),
+                P("pipe", None),
+                P("pipe", None, None),
+                P("pipe", None, None),
+                P("pipe", "dp", None, None),
+                P("pipe", "dp", None, None),
+                P("pipe", "dp", None, None),
+                P("pipe", "dp", None, None),
+                P(),
+                P(),
+                P(),
+            ),
+            out_specs=(
+                P("pipe", "dp", None, None),
+                P("pipe", "dp", None, None),
+                P("pipe", "dp", None, None),
+                P("pipe", "dp", None, None),
+            ),
+            check_vma=False,
+        )
+
+    return run

time: 581 us -> 492 us (0.85); the launches traced: 571 us -> 490 us
  waiting for transfers between devices: 76.5 us -> 329 us
  other arithmetic: 210 us -> 26.1 us
  starting transfers between devices: 81.2 us -> 14.4 us
  local copies, waits for them, and re-layouts: 108 us -> 54.9 us
  matrix products: 70.3 us -> 42.4 us
  blocking collectives: 22.2 us -> 8.12 us
  between operations: 2.1 us -> 14.6 us
    psum x0 -> x7, waiting for transfers between devices: none -> 276 us  [the longest x4 154 us: columns_body(): whole = lax.psum(partial, 'pipe')]
    unnamed x8 -> x1, other arithmetic: 181 us -> 0.06 us
    all_to_all x16 -> x3, starting transfers between devices: 72 us -> 13.9 us  [the longest x1 5.29 us: columns_body(): lax.all_to_all(jnp.stack([inputs, cotangent], axis=1), 'pipe', split_axis...]
    ppermute x14 -> x0, waiting for transfers between devices: 43 us -> none  [from_behind(): lax.ppermute(value, axis, [(i, (i + by) % peers) for i in range(peers)])]
    unnamed x37 -> x74, local copies, waits for them, and re-layouts: 34.4 us -> 13.6 us
    dot_general x28 -> x6, matrix products: 31.4 us -> 11 us  [contract_leading(): lax.dot_general(left, right, (((0,), (0,)), ((), ())), preferred_element_...]
    all_to_all x16 -> x3, waiting for transfers between devices: 33.6 us -> 53.5 us  [the longest x1 45.9 us: columns_body(): lax.all_to_all(jnp.stack([into, outof])[None], 'pipe', split_axis=3, conc...]
    squeeze x4 -> x0, local copies, waits for them, and re-layouts: 17.8 us -> none  [the longest x1 8.31 us: body(): value_down[0]]
  transfers between devices with their start and end apart: 30 -> 11, of which waited for: 15 -> 10; matrix products, arithmetic and copies ran while one was open for 58% -> 8% of each run, Pallas kernels for 0% -> 0%
where the time goes in v1:
time: 492 us; the launch traced here: 490 us
  waiting for transfers between devices  329 us (67%)
  local copies, waits for them, and re-layouts  54.9 us (11%)
  matrix products  42.4 us (9%)
  other arithmetic  26.1 us (5%)
  between operations  14.6 us (3%)
  starting transfers between devices  14.4 us (3%)
  blocking collectives  8.12 us (2%)
    psum x4, waiting for transfers between devices, columns_body(): whole = lax.psum(partial, 'pipe')  154 us
    psum x3, waiting for transfers between devices, columns_body(): back = lax.psum(trail(weights[layer, 1], gradient), 'pipe')  122 us
    all_to_all x1, waiting for transfers between devices, columns_body(): lax.all_to_all(jnp.stack([into, outof])[None], 'pipe', split_axis=3, conc...  45.9 us
    dot_general x16, matrix products, trail(): lax.dot_general(left, right, (((1,), (1,)), ((), ())), preferred_element_...  18.4 us
    unnamed x74, local copies, waits for them, and re-layouts  13.6 us
    dot_general x23, matrix products, plain(): return jnp.dot(left, right, preferred_element_type=jnp.float32)  12.9 us
    dot_general x6, matrix products, contract_leading(): lax.dot_general(left, right, (((0,), (0,)), ((), ())), preferred_element_...  11 us
    all_to_all x1, local copies, waits for them, and re-layouts, columns_body(): lax.all_to_all(jnp.stack([into, outof])[None], 'pipe', split_axis=3, conc...  10.3 us
  transfers between devices with their start and end apart: 11, of which 10 were waited for; matrix products, arithmetic and copies ran while one was open for 8% of the time, Pallas kernels for 0%

profile of v1, /device:TPU:0, one launch (start us, length us, event | category | flops | bytes accessed | tf_op | source)
XLA Modules:
  0.0 490.0 jit_solution(14800124402072414395)
XLA Ops:
  8.2 6.8 %copy.49 = bf16[1,2,8,8192]{2,1,0,3:T(2,128)(2,1)} copy(bf16[1,2,8,8192]{3,2,1,0:T(8,128)(2,1)S(1)} %pad_maximum_fusion.1) | data formatting | bytes 524288 | tf_op jit(solution)/shard_map/stack | solution.py:354
  14.9 6.5 %reshape.227 = bf16[4,2,16384]{2,1,0:T(2,128)(2,1)} reshape(bf16[8192,1,2,8]{3,2,1,0:T(2,128)(2,1)} %bitcast.219) | data formatting | bytes 524288
  21.5 5.3 %all-to-all-start.1 = ((bf16[4,2,16384]{2,1,0:T(2,128)(2,1)}), bf16[4,2,16384]{2,1,0:T(2,128)(2,1)S(1)}, u32[]{:S(2)}, u32[]{:S(2)}) async-start(bf16[4,2,16384]{2,1,0:T(2,128)(2,1)} %reshape.227), calls=%async_computation.1 | async-start | bytes 524288 | tf_op jit(solution)/shard_map/all_to_all | solution.py:353
  29.2 2.9 all-to-all-done.1
  32.1 5.9 %reshape.228 = bf16[8192,1,2,8]{3,2,1,0:T(2,128)(2,1)} reshape(bf16[4,2,16384]{2,1,0:T(2,128)(2,1)S(1)} %all-to-all-done.1) | data formatting | bytes 524288
  38.1 10.2 %copy.50 = bf16[1,2,8,4,2048]{4,2,1,0,3:T(8,128)(2,1)} copy(bf16[1,2,8,4,2048]{2,1,4,3,0:T(2,128)(2,1)} %bitcast.220) | data formatting | bytes 524288 | tf_op jit(solution)/shard_map/all_to_all | solution.py:353
  48.3 2.0 maximum_bitcast_fusion
  50.2 6.9 %copy.47 = bf16[1,2,80,8192]{2,1,0,3:T(2,128)(2,1)} copy(bf16[1,2,80,8192]{3,2,1,0:T(8,128)(2,1)S(1)} %maximum_bitcast_fusion) | data formatting | bytes 5242880 | tf_op jit(solution)/shard_map/broadcast_in_dim | solution.py:348
  57.2 5.0 %all-to-all-start = ((bf16[1,2,80,8192]{2,1,0,3:T(2,128)(2,1)}), bf16[1,2,80,8192]{2,1,0,3:T(2,128)(2,1)}, u32[]{:S(2)}, u32[]{:S(2)}) async-start(bf16[1,2,80,8192]{2,1,0,3:T(2,128)(2,1)} %copy.47), calls=%async_computation | async-start | bytes 8388608 | tf_op jit(solution)/shard_map/all_to_all | solution.py:347
  62.5 45.9 %all-to-all-done = bf16[1,2,80,8192]{2,1,0,3:T(2,128)(2,1)} async-done(((bf16[1,2,80,8192]{2,1,0,3:T(2,128)(2,1)}), bf16[1,2,80,8192]{2,1,0,3:T(2,128)(2,1)}, u32[]{:S(2)}, u32[]{:S(2)}) %all-to-all-start) | async-done | bytes 2621472 | tf_op jit(solution)/shard_map/all_to_all | solution.py:347
  108.4 10.3 %copy.56 = bf16[1,2,80,4,2048]{4,3,2,1,0:T(4,128)(2,1)S(1)} copy(bf16[1,2,80,4,2048]{2,1,4,3,0:T(2,128)(2,1)} %bitcast.6) | data formatting | bytes 5242880 | tf_op jit(solution)/shard_map/all_to_all | solution.py:347
  118.8 5.4 %fusion.156 = (bf16[1,1,80,2048]{3,0,2,1:T(2,128)(2,1)}, bf16[1,1,80,2048]{3,0,2,1:T(2,128)(2,1)}, bf16[1,1,80,2048]{3,0,2,1:T(2,128)(2,1)}, bf16[1,1,80,2048]{3...) fusion(bf16[4,2,80,2048]{3,0,2,1:T(4,128)(2,1)S(1)} %bitcast.218), kind=kLoop, calls=%fused_computation.270 | loop fusion | bytes 5242880 | tf_op jit(solution)/shard_map/slice | solution.py:383
  124.2 3.3 fusion.157
  130.2 8.1 %all-gather.1 = bf16[8,16,64]{2,1,0:T(8,128)(2,1)S(1)} all-gather(bf16[2,16,64]{2,1,0:T(8,128)(2,1)S(1)} %pad_maximum_fusion.11), channel_id=3, replica_groups=mesh['pipe'=4,'dp'=8] {'pipe'}, dimensions={0}, use_global_device_ids=true | all-gather | bytes 20480 | tf_op jit(solution)/shard_map/all_gather | solution.py:350
  138.3 34.0 %all-reduce.9.cloned.1.call-done = f32[81,256]{1,0:T(8,128)} async-done(((f32[81,256]{1,0:T(8,128)}), f32[81,256]{1,0:T(8,128)}) %all-reduce.9.cloned.1.call-update) | async-done | bytes 82960 | tf_op jit(solution)/shard_map/psum | solution.py:370
  177.3 41.8 %all-reduce.11.cloned.1.call-done = f32[81,256]{1,0:T(8,128)} async-done(((f32[81,256]{1,0:T(8,128)}), f32[81,256]{1,0:T(8,128)}) %all-reduce.11.cloned.1.call-update) | async-done | bytes 82960 | tf_op jit(solution)/shard_map/psum | solution.py:370
  222.7 1.9 fusion.58
  225.4 2.5 fusion.72
  227.9 39.4 %all-reduce.13.cloned.1.call-done = f32[81,256]{1,0:T(8,128)} async-done(((f32[81,256]{1,0:T(8,128)}), f32[81,256]{1,0:T(8,128)}) %all-reduce.13.cloned.1.call-update) | async-done | bytes 82960 | tf_op jit(solution)/shard_map/psum | solution.py:370
  269.2 1.7 fusion.21
  271.0 1.9 fusion.70
  273.8 2.7 fusion.24
  276.5 39.1 %all-reduce.21.cloned.1.call-done = (f32[81,256]{1,0:T(8,128)}, f32[80,256]{1,0:T(8,128)}) async-done(((f32[81,256]{1,0:T(8,128)}, f32[80,256]{1,0:T(8,128)}), (f32[81,256]{1,0:T(8,128)}, f32[80,256]{1,0:T(8,128)})) %all-reduce.21.cloned.1.call-update) | async-done | bytes 164880 | tf_op jit(solution)/shard_map/psum | solution.py:370
  320.6 2.1 fusion.4
  324.3 2.2 fusion.54
  328.3 40.2 %all-reduce.15.cloned.1.call-done = f32[80,256]{1,0:T(8,128)} async-done(((f32[80,256]{1,0:T(8,128)}), f32[80,256]{1,0:T(8,128)}) %all-reduce.15.cloned.1.call-update) | async-done | bytes 81936 | tf_op jit(solution)/shard_map/psum | solution.py:383
  372.2 2.1 fusion.5
  377.2 40.2 %all-reduce.17.cloned.1.call-done = f32[80,256]{1,0:T(8,128)} async-done(((f32[80,256]{1,0:T(8,128)}), f32[80,256]{1,0:T(8,128)}) %all-reduce.17.cloned.1.call-update) | async-done | bytes 81936 | tf_op jit(solution)/shard_map/psum | solution.py:383
  420.3 1.7 fusion.6
  426.5 41.1 %all-reduce.19.cloned.1.call-done = f32[80,256]{1,0:T(8,128)} async-done(((f32[80,256]{1,0:T(8,128)}), f32[80,256]{1,0:T(8,128)}) %all-reduce.19.cloned.1.call-update) | async-done | bytes 81936 | tf_op jit(solution)/shard_map/psum | solution.py:383
  470.1 3.6 all-to-all-start.2
  476.9 4.7 all-to-all-done.2
  (166 shorter events, 47.8 us)
Async XLA Ops:
  14.9 11.8 %copy-start.12 = (bf16[1,64,8192]{2,1,0:T(8,128)(2,1)S(1)}, bf16[1,64,8192]{2,1,0:T(8,128)(2,1)}, u32[]{:S(2)}) copy-start(bf16[1,64,8192]{2,1,0:T(8,128)(2,1)} %param.15) | copy-start | bytes 3145732
  14.9 11.8 %copy-start.20 = (bf16[1,1,16,8192]{3,2,1,0:T(8,128)(2,1)S(1)}, bf16[1,1,16,8192]{3,2,1,0:T(8,128)(2,1)}, u32[]{:S(2)}) copy-start(bf16[1,1,16,8192]{3,2,1,0:T(8,128)(2,1)} %param.17) | copy-start | bytes 786436
  14.9 11.8 %copy-start.24 = (f32[1,8192]{1,0:T(1,128)S(1)}, f32[1,8192]{1,0:T(1,128)}, u32[]{:S(2)}) copy-start(f32[1,8192]{1,0:T(1,128)} %param.14) | copy-start | bytes 98308
  21.4 6.6 %copy-start.11 = (bf16[1,64,8192]{2,1,0:T(8,128)(2,1)S(1)}, bf16[1,64,8192]{2,1,0:T(8,128)(2,1)}, u32[]{:S(2)}) copy-start(bf16[1,64,8192]{2,1,0:T(8,128)(2,1)} %param.16) | copy-start | bytes 3145732
  21.4 6.6 %copy-start.15 = (bf16[1,1,16,8192]{3,2,1,0:T(8,128)(2,1)S(1)}, bf16[1,1,16,8192]{3,2,1,0:T(8,128)(2,1)}, u32[]{:S(2)}) copy-start(bf16[1,1,16,8192]{3,2,1,0:T(8,128)(2,1)} %param.20) | copy-start | bytes 786436
  21.5 10.7 %all-to-all-start.1 = ((bf16[4,2,16384]{2,1,0:T(2,128)(2,1)}), bf16[4,2,16384]{2,1,0:T(2,128)(2,1)S(1)}, u32[]{:S(2)}, u32[]{:S(2)}) async-start(bf16[4,2,16384]{2,1,0:T(2,128)(2,1)} %reshape.227), calls=%async_computation.1 | async-start | bytes 524288 | tf_op jit(solution)/shard_map/all_to_all | solution.py:353
  26.7 97.4 %all-gather.4.cloned.1.call-start = ((), (), s32[]{:S(2)}) async-start(), calls=%async_computation.9 | async-start | bytes 2359296 | tf_op jit(solution)/shard_map/all_gather | solution.py:356
  57.2 5.0 %copy-start.34 = (s32[8]{0:T(128)S(1)}, s32[8]{0:T(128)}, u32[]{:S(2)}) copy-start(s32[8]{0:T(128)} %param.21) | copy-start | bytes 100
  57.2 5.1 %copy-start.35 = (s32[8]{0:T(128)S(1)}, s32[8]{0:T(128)}, u32[]{:S(2)}) copy-start(s32[8]{0:T(128)} %param.23) | copy-start | bytes 100
  57.2 51.2 %all-to-all-start = ((bf16[1,2,80,8192]{2,1,0,3:T(2,128)(2,1)}), bf16[1,2,80,8192]{2,1,0,3:T(2,128)(2,1)}, u32[]{:S(2)}, u32[]{:S(2)}) async-start(bf16[1,2,80,8192]{2,1,0,3:T(2,128)(2,1)} %copy.47), calls=%async_computation | async-start | bytes 8388608 | tf_op jit(solution)/shard_map/all_to_all | solution.py:347
  62.2 110.1 %all-reduce.9.cloned.1.call-start = ((), (), s32[]{:S(2)}) async-start(), calls=%async_computation.3 | async-start | bytes 180224 | tf_op jit(solution)/shard_map/psum | solution.py:370
  128.9 46.9 %copy-start.7 = (bf16[1,1,80,2048]{3,0,2,1:T(2,128)(2,1)S(1)}, bf16[1,1,80,2048]{3,0,2,1:T(2,128)(2,1)}, u32[]{:S(2)}) copy-start(bf16[1,1,80,2048]{3,0,2,1:T(2,128)(2,1)} %get-tuple-element.14) | copy-start | bytes 983044
  130.1 89.0 %all-reduce.11.cloned.1.call-start = ((), (), s32[]{:S(2)}) async-start(), calls=%async_computation.4 | async-start | bytes 180224 | tf_op jit(solution)/shard_map/psum | solution.py:370
  175.9 46.8 %copy-start = (bf16[256,2048]{1,0:T(8,128)(2,1)}, bf16[256,2048]{1,0:T(8,128)(2,1)S(1)}, u32[]{:S(2)}) copy-start(bf16[256,2048]{1,0:T(8,128)(2,1)S(1)} %get-tuple-element.33) | copy-start | bytes 3145732
  177.1 90.3 %all-reduce.13.cloned.1.call-start = ((), (), s32[]{:S(2)}) async-start(), calls=%async_computation.5 | async-start | bytes 180224 | tf_op jit(solution)/shard_map/psum | solution.py:370
  222.7 148.6 %copy-start.2 = (bf16[256,2048]{1,0:T(8,128)(2,1)}, bf16[256,2048]{1,0:T(8,128)(2,1)S(1)}, u32[]{:S(2)}) copy-start(bf16[256,2048]{1,0:T(8,128)(2,1)S(1)} %get-tuple-element.37) | copy-start | bytes 3145732
  225.3 90.3 %all-reduce.21.cloned.1.call-start = ((), (), s32[]{:S(2)}) async-start(), calls=%async_computation.10 | async-start | bytes 344064 | tf_op jit(solution)/shard_map/psum | solution.py:370
  270.9 49.4 %copy-start.3 = (bf16[256,2048]{1,0:T(8,128)(2,1)}, bf16[256,2048]{1,0:T(8,128)(2,1)S(1)}, u32[]{:S(2)}) copy-start(bf16[256,2048]{1,0:T(8,128)(2,1)S(1)} %get-tuple-element.41) | copy-start | bytes 3145732
  273.6 94.9 %all-reduce.15.cloned.1.call-start = ((), (), s32[]{:S(2)}) async-start(), calls=%async_computation.6 | async-start | bytes 163840 | tf_op jit(solution)/shard_map/psum | solution.py:383
  322.7 47.8 %copy-start.14 = (f32[81,256]{1,0:T(8,128)S(1)}, f32[81,256]{1,0:T(8,128)}, u32[]{:S(2)}) copy-start(f32[81,256]{1,0:T(8,128)} %all-reduce.13.cloned.1.call-done) | copy-start | bytes 248836
  326.6 90.9 %all-reduce.17.cloned.1.call-start = ((), (), s32[]{:S(2)}) async-start(), calls=%async_computation.7 | async-start | bytes 163840 | tf_op jit(solution)/shard_map/psum | solution.py:383
  374.3 44.4 %copy-start.13 = (f32[81,256]{1,0:T(8,128)S(1)}, f32[81,256]{1,0:T(8,128)}, u32[]{:S(2)}) copy-start(f32[81,256]{1,0:T(8,128)} %all-reduce.11.cloned.1.call-done) | copy-start | bytes 248836
  374.3 45.1 %copy-start.1 = (bf16[256,2048]{1,0:T(8,128)(2,1)S(1)}, bf16[256,2048]{1,0:T(8,128)(2,1)}, u32[]{:S(2)}) copy-start(bf16[256,2048]{1,0:T(8,128)(2,1)} %copy-done) | copy-start | bytes 3145732
  375.5 92.2 %all-reduce.19.cloned.1.call-start = ((), (), s32[]{:S(2)}) async-start(), calls=%async_computation.8 | async-start | bytes 163840 | tf_op jit(solution)/shard_map/psum | solution.py:383
  423.0 45.8 %copy-start.30 = (f32[1,256]{1,0:T(1,128)S(1)}, f32[1,256]{1,0:T(1,128)}, u32[]{:S(2)}) copy-start(f32[1,256]{1,0:T(1,128)} %copy-done.29) | copy-start | bytes 3076
  423.0 46.1 %copy-start.16 = (bf16[1,16,2048]{2,1,0:T(8,128)(2,1)S(1)}, bf16[1,16,2048]{2,1,0:T(8,128)(2,1)}, u32[]{:S(2)}) copy-start(bf16[1,16,2048]{2,1,0:T(8,128)(2,1)} %fusion.18) | copy-start | bytes 196612
  423.0 46.1 %copy-start.17 = (bf16[1,16,2048]{2,1,0:T(8,128)(2,1)S(1)}, bf16[1,16,2048]{2,1,0:T(8,128)(2,1)}, u32[]{:S(2)}) copy-start(bf16[1,16,2048]{2,1,0:T(8,128)(2,1)} %fusion.15) | copy-start | bytes 196612
  423.0 46.1 %copy-start.18 = (bf16[1,16,2048]{2,1,0:T(8,128)(2,1)S(1)}, bf16[1,16,2048]{2,1,0:T(8,128)(2,1)}, u32[]{:S(2)}) copy-start(bf16[1,16,2048]{2,1,0:T(8,128)(2,1)} %fusion.19) | copy-start | bytes 196612
  423.0 46.1 %copy-start.19 = (bf16[1,16,2048]{2,1,0:T(8,128)(2,1)S(1)}, bf16[1,16,2048]{2,1,0:T(8,128)(2,1)}, u32[]{:S(2)}) copy-start(bf16[1,16,2048]{2,1,0:T(8,128)(2,1)} %fusion.14) | copy-start | bytes 196612
  469.1 7.1 %copy-start.26 = (bf16[1,16,64]{2,1,0:T(8,128)(2,1)S(1)}, bf16[1,16,64]{2,1,0:T(8,128)(2,1)}, u32[]{:S(2)}) copy-start(bf16[1,16,64]{2,1,0:T(8,128)(2,1)} %fusion.49) | copy-start | bytes 6148
  470.1 12.4 %copy-start.25 = (f32[1,8192]{1,0:T(1,128)S(1)}, f32[1,8192]{1,0:T(1,128)}, u32[]{:S(2)}) copy-start(f32[1,8192]{1,0:T(1,128)} %param.14) | copy-start | bytes 98308
  470.1 11.5 %all-to-all-start.2 = ((bf16[4,2,16,2048]{3,2,1,0:T(8,128)(2,1)}), bf16[4,2,16,2048]{3,2,1,0:T(8,128)(2,1)S(1)}, u32[]{:S(2)}, u32[]{:S(2)}) async-start(bf16[4,2,16,2048]{3,2,1,0:T(8,128)(2,1)} %copy.53), calls=%async_computation.2 | async-start | bytes 1048576 | tf_op jit(solution)/shard_map/all_to_all | solution.py:402
  (15 other events, 51.4 us)
Sparse Core Ops, SparseCore 0:
  48.4 29.1 all-gather.3
  130.2 41.9 all-reduce.8
  177.2 41.8 all-reduce.10
  225.4 41.8 all-reduce.12
  273.7 41.9 all-reduce.20
  326.7 41.7 all-reduce.14
  375.6 41.8 all-reduce.16
  425.8 41.8 all-reduce.18

commit v2 on v1

--- a/solution.py
+++ b/solution.py
@@ -1,6 +1,10 @@
+import functools
+
 import jax
 import jax.numpy as jnp
 from jax import lax
+from jax.experimental import pallas as pl
+from jax.experimental.pallas import tpu as pltpu
 from jax.sharding import PartitionSpec as P
 
 adapter_scale = 2.0
@@ -304,24 +308,450 @@
     return jnp.where(keep, 1.0, 0.0).astype(jnp.float32) / tokens[:, None]
 
 
-def forward_small(projection, inverse, up_turned, out_down):
-    hd = projection.shape[0] - out_down.shape[0]
-    scaled = projection * inverse
-    lowrank = scaled[hd:].astype(jnp.bfloat16)
-    value = (scaled[:hd] + adapter_scale * plain(up_turned, lowrank)).astype(jnp.bfloat16)
-    side = plain(out_down, value).astype(jnp.bfloat16)
-    return lowrank, value, side
-
-
-def backward_small(back, up_factor, down_turned):
-    hd = up_factor.shape[1]
-    grad_side = (adapter_scale * back[hd:]).astype(jnp.bfloat16)
-    grad_value = (back[:hd] + plain(down_turned, grad_side)).astype(jnp.bfloat16)
-    grad_low = (adapter_scale * plain(up_factor, grad_value)).astype(jnp.bfloat16)
-    return grad_side, grad_value, grad_low
-
-
-def columns_body(
+def columns_kernel(
+    shape,
+    tok,
+    wts,
+    fac,
+    row_weight,
+    gain,
+    out_vd,
+    out_vu,
+    out_od,
+    out_ou,
+    hid,
+    grad,
+    cot,
+    tbuf,
+    pbuf,
+    qbuf,
+    fbuf,
+    turned,
+    land,
+    mine,
+    fx_out,
+    fx_in,
+    bx_out,
+    bx_in,
+    local_sem,
+    tok_sem,
+    fac_sem,
+    p_sem,
+    q_sem,
+    psib_sem,
+    qsib_sem,
+    x_up,
+    x_down,
+    x_sib,
+    c_up,
+    c_down,
+    c_sib,
+    fx_sem,
+    bx_sem,
+    land_sem,
+):
+    sections, members = shape
+    levels = members // 2
+    section, member = lax.axis_index("pipe"), lax.axis_index("dp")
+    core, level = lax.rem(member, 2), lax.div(member, 2)
+    sibling = (section, member + 1 - 2 * core)
+    row_total, columns = hid.shape[1:]
+    block = row_total // members
+    width = columns * sections
+    hd, rank = wts.shape[0] // 2 - out_vu.shape[0], out_vu.shape[0]
+    half, ranks = hd // 2, wts.shape[0] // 2
+    peers = [lax.rem(section + j, sections) for j in range(1, sections)]
+    step = min(512, columns)
+    chunks = columns // step
+
+    def remote(src, dst, sem, slot, target, got=None):
+        return pltpu.make_async_remote_copy(
+            src_ref=src,
+            dst_ref=dst,
+            send_sem=sem.at[0, slot],
+            recv_sem=sem.at[1, slot if got is None else got],
+            device_id=target,
+            device_id_type=pl.DeviceIdType.MESH,
+        )
+
+    barrier = pltpu.get_barrier_semaphore()
+    greeted = [(q, member) for q in peers] + [sibling]
+    greeted += [(section, lax.rem(member + by, members)) for by in (2, members - 2)]
+    for target in greeted:
+        pl.semaphore_signal(
+            barrier, inc=1, device_id=target, device_id_type=pl.DeviceIdType.MESH
+        )
+    own_columns = pl.ds(pl.multiple_of(section * columns, columns), columns)
+    local = [
+        pltpu.make_async_copy(tok.at[:, own_columns], tbuf.at[section], local_sem.at[0]),
+        pltpu.make_async_copy(fac, fbuf.at[section], local_sem.at[1]),
+        pltpu.make_async_copy(
+            wts.at[pl.ds(0, ranks), own_columns], pbuf.at[section], local_sem.at[2]
+        ),
+        pltpu.make_async_copy(
+            wts.at[pl.ds(ranks, ranks), own_columns], qbuf.at[section], local_sem.at[3]
+        ),
+    ]
+    for copy in local:
+        copy.start()
+    pl.semaphore_wait(barrier, len(greeted))
+
+    share = half + rank
+    share_rows = pl.ds(pl.multiple_of(core * half, 16), share)
+    out_rows = pl.ds(pl.multiple_of(ranks + core * half, 16), share)
+    pass_rows = pl.ds(pl.multiple_of(core * share, 16), half)
+
+    def to_columns(q):
+        return pl.ds(pl.multiple_of(q * columns, columns), columns)
+
+    def tok_copy(j, src_section):
+        q = peers[j]
+        return remote(
+            tok.at[:, to_columns(q)], tbuf.at[src_section], tok_sem, j, (q, member), src_section
+        )
+
+    def fac_copy(j, src_section):
+        return remote(fac, fbuf.at[src_section], fac_sem, j, (peers[j], member), src_section)
+
+    def p_copy(j, src_section):
+        q = peers[j]
+        return remote(
+            wts.at[share_rows, to_columns(q)],
+            pbuf.at[src_section, share_rows],
+            p_sem,
+            j,
+            (q, member),
+            src_section,
+        )
+
+    def q_copy(j, src_section):
+        q = peers[j]
+        return remote(
+            wts.at[out_rows, to_columns(q)],
+            qbuf.at[src_section, share_rows],
+            q_sem,
+            j,
+            (q, member),
+            src_section,
+        )
+
+    def sib_weight(buf, sem, layer):
+        piece = buf.at[layer, pass_rows]
+        return remote(piece, piece, sem, layer, sibling)
+
+    def arrive(copy_of, layer):
+        @pl.when(section != layer)
+        def _():
+            copy_of(0, layer).wait_recv()
+
+    def arrive_and_pass(copy_of, buf, sem, layer):
+        @pl.when(section != layer)
+        def _():
+            copy_of(0, layer).wait_recv()
+            sib_weight(buf, sem, layer).start()
+
+    def passed(buf, sem, layer):
+        @pl.when(section != layer)
+        def _():
+            sib_weight(buf, sem, layer).wait_recv()
+
+    def block_rows(buf, at_level):
+        start = pl.multiple_of((at_level * 2 + core) * block, block)
+        return buf.at[pl.ds(start, block)]
+
+    def up_copy(buf, sem, k):
+        piece = block_rows(buf, level - k)
+        return remote(piece, piece, sem, k, (section, member + 2))
+
+    def down_copy(buf, sem, k):
+        piece = block_rows(buf, level + k)
+        return remote(piece, piece, sem, k, (section, member - 2))
+
+    def sib_copy(buf, sem, at_level):
+        piece = block_rows(buf, at_level)
+        return remote(piece, piece, sem, at_level, sibling)
+
+    def line_start(buf, up, down, k):
+        @pl.when((level < levels - 1) & (level - k >= 0))
+        def _():
+            up_copy(buf, up, k).start()
+
+        @pl.when((level > 0) & (level + k < levels))
+        def _():
+            down_copy(buf, down, k).start()
+
+    def line_arrive(buf, up, down, sib, k):
+        @pl.when(level - 1 - k >= 0)
+        def _():
+            up_copy(buf, up, k).wait_recv()
+
+        @pl.when(level + 1 + k < levels)
+        def _():
+            down_copy(buf, down, k).wait_recv()
+
+        if k + 1 < levels - 1:
+            line_start(buf, up, down, k + 1)
+
+        @pl.when(level - 1 - k >= 0)
+        def _():
+            sib_copy(buf, sib, level - 1 - k).start()
+
+        @pl.when(level + 1 + k < levels)
+        def _():
+            sib_copy(buf, sib, level + 1 + k).start()
+
+    def line_sent(buf, up, down, sib):
+        for k in range(levels - 1):
+
+            @pl.when((level < levels - 1) & (level - k >= 0))
+            def _(k=k):
+                up_copy(buf, up, k).wait_send()
+
+            @pl.when((level > 0) & (level + k < levels))
+            def _(k=k):
+                down_copy(buf, down, k).wait_send()
+
+        for at_level in range(levels):
+            sib_copy(buf, sib, at_level).wait_send()
+
+    def sum_copy(out, into, sem, layer, j):
+        return remote(
+            out.at[layer],
+            into.at[layer, j],
+            sem,
+            layer * (sections - 1) + j,
+            (peers[j], member),
+        )
+
+    def send_sum(out, into, sem, layer, partial):
+        out[layer] = partial.astype(jnp.bfloat16)
+        for j in range(sections - 1):
+            sum_copy(out, into, sem, layer, j).start()
+
+    def whole_sum(out, into, sem, layer, partial):
+        for j in range(sections - 1):
+            sum_copy(out, into, sem, layer, j).wait_recv()
+        for j in range(sections - 1):
+            partial = partial + into[layer, j].astype(jnp.float32)
+        return partial
+
+    for j in range(sections - 1):
+        tok_copy(j, section).start()
+    for j in range(sections - 1):
+        p_copy(j, section).start()
+    for j in range(sections - 1):
+        fac_copy(j, section).start()
+
+    local[0].wait()
+    for layer in range(sections):
+        arrive(tok_copy, layer)
+    per = block // sections
+    for t in range(chunks):
+        at = pl.ds(t * step, step)
+        wide = [tbuf[m, :, at].astype(jnp.float32) for m in range(sections)]
+        own = pl.ds(pl.multiple_of(member * block, block), block)
+        hid[0, own, at] = jnp.concatenate([w[:per] for w in wide]).astype(jnp.bfloat16)
+        cot[own, at] = jnp.concatenate([w[per:] for w in wide]).astype(jnp.bfloat16)
+    x0 = hid.at[0]
+    line_start(x0, x_up, x_down, 0)
+    sib_copy(x0, x_sib, level).start()
+    for j in range(sections - 1):
+        q_copy(j, section).start()
+    for k in range(levels - 1):
+        line_arrive(x0, x_up, x_down, x_sib, k)
+    line_start(cot, c_up, c_down, 0)
+    sib_copy(cot, c_sib, level).start()
+    for copy in local[1:]:
+        copy.wait()
+    for layer in range(sections):
+        arrive_and_pass(p_copy, pbuf, psib_sem, layer)
+        arrive(fac_copy, layer)
+    for at_level in range(levels):
+        sib_copy(x0, x_sib, at_level).wait_recv()
+
+    ones = jnp.ones((16, step), jnp.bfloat16)
+
+    def chunk(t):
+        return pl.ds(pl.multiple_of(t * step, step), step)
+
+    def project(layer, at, rows):
+        squares = (rows.astype(jnp.float32) * rows.astype(jnp.float32)).astype(jnp.bfloat16)
+        return trail(pbuf[layer, :, at], rows), trail(ones, squares)
+
+    def add(left, right):
+        return tuple(a + b for a, b in zip(left, right))
+
+    zero_sum = (
+        jnp.zeros((ranks, row_total), jnp.float32),
+        jnp.zeros((16, row_total), jnp.float32),
+    )
+
+    def turn(parts):
+        parts = jnp.concatenate(parts)
+        spare = jnp.zeros((128 - parts.shape[0], row_total), jnp.float32)
+        return jnp.concatenate([parts, spare]).T
+
+    def first(t, total):
+        return add(total, project(0, chunk(t), hid[0, :, chunk(t)]))
+
+    passed(pbuf, psib_sem, 0)
+    total = lax.fori_loop(0, chunks, first, zero_sum)
+    kept = []
+    last = sections - 1
+    back = None
+    for layer in range(sections):
+        squares = total[1][:8]
+        high = squares.astype(jnp.bfloat16).astype(jnp.float32)
+        partial = jnp.concatenate([total[0], high, squares - high])
+        send_sum(fx_out, fx_in, fx_sem, layer, partial)
+        if layer < levels - 1:
+            line_arrive(cot, c_up, c_down, c_sib, layer)
+        if layer == 0:
+            arrive_and_pass(q_copy, qbuf, qsib_sem, 0)
+            passed(qbuf, qsib_sem, 0)
+        if layer == 1:
+            for later in range(1, sections):
+                arrive_and_pass(q_copy, qbuf, qsib_sem, later)
+        if 0 < layer:
+            passed(qbuf, qsib_sem, layer)
+        if layer < last:
+            passed(pbuf, psib_sem, layer + 1)
+        if layer == last:
+            for k in range(last + 1, levels - 1):
+                line_arrive(cot, c_up, c_down, c_sib, k)
+            for at_level in range(levels):
+                sib_copy(cot, c_sib, at_level).wait_recv()
+
+            def seed(t, total_now):
+                at = chunk(t)
+                top = (cot[:, at].astype(jnp.float32) * row_weight[...]).astype(jnp.bfloat16)
+                grad[last, :, at] = top
+                return total_now + trail(qbuf[last, :, at], top)
+
+            back = lax.fori_loop(0, chunks, seed, zero_sum[0])
+            send_sum(bx_out, bx_in, bx_sem, last, back)
+        whole = whole_sum(fx_out, fx_in, fx_sem, layer, partial)
+        projection = whole[:ranks]
+        inverse = lax.rsqrt((whole[ranks : ranks + 1] + whole[ranks + 8 : ranks + 9]) / width + norm_eps)
+        factor = fbuf[layer]
+        scaled = projection * inverse
+        lowrank = scaled[half : half + rank].astype(jnp.bfloat16)
+        straight = jnp.concatenate([scaled[:half], scaled[half + rank :]])
+        value = (
+            straight + adapter_scale * plain(factor[rank:, :rank], lowrank)
+        ).astype(jnp.bfloat16)
+        side = plain(factor[:rank, hd : 2 * hd], value).astype(jnp.bfloat16)
+        kept.append((projection, inverse, lowrank, value, side))
+        if layer < last:
+            wide_value = value.astype(jnp.float32)
+            mixed = [
+                wide_value[:half],
+                adapter_scale * side.astype(jnp.float32),
+                wide_value[half:],
+            ]
+            turned[...] = turn(mixed).astype(jnp.bfloat16)
+
+            def update(t, total_now, layer=layer):
+                at = chunk(t)
+                rows = hid[layer, :, at].astype(jnp.float32)
+                rows = rows + plain(turned[:, :ranks], qbuf[layer, :, at])
+                rows = rows.astype(jnp.bfloat16)
+                hid[layer + 1, :, at] = rows
+                return add(total_now, project(layer + 1, at, rows))
+
+            total = lax.fori_loop(0, chunks, update, zero_sum)
+
+    for layer in reversed(range(sections)):
+        projection, inverse, lowrank, value, side = kept[layer]
+        factor = fbuf[layer]
+        whole = whole_sum(bx_out, bx_in, bx_sem, layer, back)
+        grad_side = (adapter_scale * whole[half : half + rank]).astype(jnp.bfloat16)
+        straight = jnp.concatenate([whole[:half], whole[half + rank :]])
+        grad_value = (straight + plain(factor[rank:, hd : hd + rank], grad_side)).astype(
+            jnp.bfloat16
+        )
+        grad_low = (adapter_scale * plain(factor[:rank, :hd], grad_value)).astype(jnp.bfloat16)
+        wide_value = grad_value.astype(jnp.float32)
+        both = jnp.concatenate(
+            [wide_value[:half], grad_low.astype(jnp.float32), wide_value[half:]]
+        )
+        scaled = both * inverse
+        if layer > 0:
+            correction = jnp.sum(both * projection, axis=0, keepdims=True) / width
+            shrink = inverse * inverse * inverse * correction
+            shrink = jnp.broadcast_to(shrink, (8, row_total))
+            columns_of = turn([scaled, shrink])
+            turned[...] = columns_of.astype(jnp.bfloat16)
+            shrink_column = columns_of[:, ranks : ranks + 1]
+
+            def step_back(t, total_now, layer=layer, shrink_column=shrink_column):
+                at = chunk(t)
+                rows = hid[layer, :, at].astype(jnp.float32)
+                fresh = grad[layer, :, at].astype(jnp.float32)
+                fresh = fresh + plain(turned[:, :ranks], pbuf[layer, :, at])
+                fresh = (fresh - rows * shrink_column).astype(jnp.bfloat16)
+                grad[layer - 1, :, at] = fresh
+                return total_now + trail(qbuf[layer - 1, :, at], fresh)
+
+            back = lax.fori_loop(0, chunks, step_back, zero_sum[0])
+            send_sum(bx_out, bx_in, bx_sem, layer - 1, back)
+        low_scaled = scaled[half : half + rank].astype(jnp.bfloat16)
+
+        def gather(t, carry, layer=layer, low_scaled=low_scaled, side=side):
+            at = chunk(t)
+            mine[layer, 0, :, at] = plain(low_scaled, hid[layer, :, at]).astype(jnp.bfloat16)
+            mine[layer, 1, :, at] = (
+                adapter_scale * plain(side, grad[layer, :, at])
+            ).astype(jnp.bfloat16)
+            return carry
+
+        lax.fori_loop(0, chunks, gather, 0)
+        land_copy = remote(
+            mine.at[layer], land.at[section], land_sem, layer, (layer, member), section
+        )
+
+        @pl.when(section != layer)
+        def _(land_copy=land_copy):
+            land_copy.start()
+
+        @pl.when(section == layer)
+        def _(layer=layer, lowrank=lowrank, grad_value=grad_value, grad_side=grad_side, value=value):
+            land[layer] = mine[layer]
+            out_vu[...] = (adapter_scale * trail(lowrank, grad_value)).astype(jnp.bfloat16)
+            out_od[...] = trail(grad_side, value).astype(jnp.bfloat16)
+
+    for source in range(sections):
+
+        @pl.when(section != source)
+        def _(source=source):
+            remote(
+                mine.at[source], land.at[source], land_sem, source, (source, member), source
+            ).wait()
+
+    for q in range(sections):
+        at = pl.ds(q * columns, columns)
+        out_vd[:, at] = (land[q, 0].astype(jnp.float32) * gain[:, at]).astype(jnp.bfloat16)
+        out_ou[:, at] = land[q, 1]
+    for j in range(sections - 1):
+        tok_copy(j, section).wait_send()
+        fac_copy(j, section).wait_send()
+        p_copy(j, section).wait_send()
+        q_copy(j, section).wait_send()
+        for layer in range(sections):
+            sum_copy(fx_out, fx_in, fx_sem, layer, j).wait_send()
+            sum_copy(bx_out, bx_in, bx_sem, layer, j).wait_send()
+    for layer in range(sections):
+
+        @pl.when(section != layer)
+        def _(layer=layer):
+            sib_weight(pbuf, psib_sem, layer).wait_send()
+            sib_weight(qbuf, qsib_sem, layer).wait_send()
+
+    line_sent(x0, x_up, x_down, x_sib)
+    line_sent(cot, c_up, c_down, c_sib)
+
+
+def kernel_body(
     inputs,
     cotangent,
     norm_gain,
@@ -335,80 +765,91 @@
     valid_tokens,
     tenant_slot,
 ):
-    section = lax.axis_index("pipe")
-    sections = lax.axis_size("pipe")
+    sections, members = lax.axis_size("pipe"), lax.axis_size("dp")
     member = lax.axis_index("dp")
     row_count, width = inputs.shape[1:]
     micro_count = inputs.shape[0] * sections
+    columns, row_total = width // sections, micro_count * row_count * members
+    rank, hd = value_up_factor.shape[2:]
+    half, ranks = hd // 2, hd + rank
     gain = norm_gain[0][None]
-    into = jnp.concatenate([w_value[0], value_down[0, 0]]).astype(jnp.float32) * gain
-    into = into.astype(jnp.bfloat16)
-    outof = jnp.concatenate([w_out[0], output_up_factor[0, 0]])
-    weights = lax.all_to_all(
-        jnp.stack([into, outof])[None], "pipe", split_axis=3, concat_axis=0, tiled=True
-    )
-    factors = lax.all_gather(
-        jnp.stack([value_up_factor[0, 0], out_down[0, 0]]), "pipe", axis=0
-    )
-    tokens = lax.all_to_all(
-        jnp.stack([inputs, cotangent], axis=1), "pipe", split_axis=3, concat_axis=0, tiled=True
-    )
-    tokens = lax.all_gather(tokens, "dp", axis=0)
-    columns = tokens.shape[-1]
-    rows = tokens[:, :, 0].reshape(-1, columns)
+
+    def folded(rows):
+        return (rows.astype(jnp.float32) * gain).astype(jnp.bfloat16)
+
+    wts = jnp.concatenate(
+        [
+            folded(w_value[0, :half]),
+            folded(value_down[0, 0]),
+            folded(w_value[0, half:]),
+            w_out[0, :half],
+            output_up_factor[0, 0],
+            w_out[0, half:],
+        ]
+    )
+    tok = jnp.concatenate([inputs[0], cotangent[0]])
+    up, down = value_up_factor[0, 0], out_down[0, 0]
+    pad = ((0, 0), (0, hd - rank))
+    fac = jnp.concatenate(
+        [
+            jnp.concatenate([up, down], axis=1),
+            jnp.concatenate([jnp.pad(up.T, pad), jnp.pad(down.T, pad)], axis=1),
+        ]
+    )
     weight = row_weights(
         block_tenant, valid_tokens, tenant_slot, member, micro_count, row_count
     ).reshape(-1, 1)
-    gradient = (tokens[:, :, 1].reshape(-1, columns).astype(jnp.float32) * weight).astype(
-        jnp.bfloat16
-    )
-    kept = []
-    for layer in range(sections):
-        wide = rows.astype(jnp.float32)
-        squares = jnp.sum(wide * wide, axis=1)[None]
-        partial = jnp.concatenate([trail(weights[layer, 0], rows), squares])
-        whole = lax.psum(partial, "pipe")
-        projection = whole[:-1]
-        inverse = lax.rsqrt(whole[-1:] / width + norm_eps)
-        lowrank, value, side = forward_small(
-            projection, inverse, factors[layer, 0].T, factors[layer, 1]
-        )
-        kept.append((rows, projection, inverse, lowrank, value, side))
-        if layer < sections - 1:
-            mixed = jnp.concatenate([value, adapter_scale * side])
-            rows = (wide + contract_leading(mixed, weights[layer, 1])).astype(jnp.bfloat16)
-    downs, ups, small_ups, small_downs = [], [], [], []
-    for layer in reversed(range(sections)):
-        rows, projection, inverse, lowrank, value, side = kept[layer]
-        back = lax.psum(trail(weights[layer, 1], gradient), "pipe")
-        grad_side, grad_value, grad_low = backward_small(
-            back, factors[layer, 0], factors[layer, 1].T
-        )
-        both = jnp.concatenate([grad_value, grad_low]).astype(jnp.float32)
-        correction = jnp.sum(both * projection, axis=0, keepdims=True) / width
-        scaled = (both * inverse).astype(jnp.bfloat16)
-        downs.append(plain(scaled[value.shape[0] :], rows).astype(jnp.bfloat16))
-        ups.append((adapter_scale * plain(side, gradient)).astype(jnp.bfloat16))
-        small_ups.append((adapter_scale * trail(lowrank, grad_value)).astype(jnp.bfloat16))
-        small_downs.append(trail(grad_side, value).astype(jnp.bfloat16))
-        if layer > 0:
-            shrink = (inverse * inverse * inverse * correction).reshape(-1, 1)
-            gradient = (
-                gradient.astype(jnp.float32)
-                + contract_leading(scaled, weights[layer, 0])
-                - rows.astype(jnp.float32) * shrink
-            ).astype(jnp.bfloat16)
-    wide_pair = jnp.stack([jnp.stack(downs[::-1]), jnp.stack(ups[::-1])], axis=1)
-    wide_pair = lax.all_to_all(wide_pair, "pipe", split_axis=0, concat_axis=3, tiled=True)[0]
-    value_down_grad = (wide_pair[0].astype(jnp.float32) * gain).astype(jnp.bfloat16)
-    own_up = lax.dynamic_index_in_dim(jnp.stack(small_ups[::-1]), section, 0, keepdims=False)
-    own_down = lax.dynamic_index_in_dim(jnp.stack(small_downs[::-1]), section, 0, keepdims=False)
-    return (
-        value_down_grad[None, None],
-        own_up[None, None],
-        own_down[None, None],
-        wide_pair[1][None, None],
-    )
+    half_type, levels = jnp.bfloat16, members // 2
+    dma = pltpu.SemaphoreType.DMA
+    vmem, anywhere = pl.BlockSpec(memory_space=pltpu.VMEM), pl.BlockSpec(memory_space=pl.ANY)
+    sums = sections * (sections - 1)
+    outs = pl.pallas_call(
+        functools.partial(columns_kernel, (sections, members)),
+        out_shape=(
+            jax.ShapeDtypeStruct((rank, width), half_type),
+            jax.ShapeDtypeStruct((rank, hd), half_type),
+            jax.ShapeDtypeStruct((rank, hd), half_type),
+            jax.ShapeDtypeStruct((rank, width), half_type),
+        ),
+        in_specs=[anywhere, anywhere, anywhere, vmem, vmem],
+        out_specs=(vmem, vmem, vmem, vmem),
+        scratch_shapes=[
+            pltpu.VMEM((sections, row_total, columns), half_type),
+            pltpu.VMEM((sections, row_total, columns), half_type),
+            pltpu.VMEM((row_total, columns), half_type),
+            pltpu.VMEM((sections, 2 * row_count, columns), half_type),
+            pltpu.VMEM((sections, ranks, columns), half_type),
+            pltpu.VMEM((sections, ranks, columns), half_type),
+            pltpu.VMEM((sections,) + fac.shape, half_type),
+            pltpu.VMEM((row_total, 128), half_type),
+            pltpu.VMEM((sections, 2, rank, columns), half_type),
+            pltpu.VMEM((sections, 2, rank, columns), half_type),
+            pltpu.VMEM((sections, ranks + 16, row_total), half_type),
+            pltpu.VMEM((sections, sections - 1, ranks + 16, row_total), half_type),
+            pltpu.VMEM((sections, ranks, row_total), half_type),
+            pltpu.VMEM((sections, sections - 1, ranks, row_total), half_type),
+            dma((4,)),
+            dma((2, sections)),
+            dma((2, sections)),
+            dma((2, sections)),
+            dma((2, sections)),
+            dma((2, sections)),
+            dma((2, sections)),
+            dma((2, levels)),
+            dma((2, levels)),
+            dma((2, levels)),
+            dma((2, levels)),
+            dma((2, levels)),
+            dma((2, levels)),
+            dma((2, sums)),
+            dma((2, sums)),
+            dma((2, sections)),
+        ],
+        compiler_params=pltpu.CompilerParams(
+            collective_id=0, has_side_effects=True, vmem_limit_bytes=50 * 2**20
+        ),
+    )(tok, wts, fac, weight, gain)
+    return tuple(part[None, None] for part in outs)
 
 
 def solution(mesh):
@@ -417,7 +858,7 @@
     def run(*arrays):
         depth, row_total, width = arrays[0].shape
         kept_bytes = 2 * depth * row_total * (width // sections) * sections
-        chosen = columns_body if kept_bytes <= stash_limit else relay_body
+        chosen = kernel_body if kept_bytes <= stash_limit else relay_body
         return place(chosen)(*arrays)
 
     def place(chosen):

time: 492 us -> 88.4 us (0.18)
  waiting for transfers between devices: 329 us -> 0 us
  Pallas kernels: 0 us -> 80.5 us
  local copies, waits for them, and re-layouts: 54.9 us -> 3.06 us
  matrix products: 42.4 us -> 0 us
  other arithmetic: 26.1 us -> 3.78 us
  starting transfers between devices: 14.4 us -> 0 us
  between operations: 14.6 us -> 0.85 us
  blocking collectives: 8.12 us -> 0 us
    psum x7 -> x0, waiting for transfers between devices: 276 us -> none  [the longest x4 154 us: columns_body(): whole = lax.psum(partial, 'pipe')]
    pallas_call x0 -> x1, Pallas kernels: none -> 80.5 us  [kernel_body(): pl.pallas_call(functools.partial(columns_kernel, (sections, members)), ou...]
    all_to_all x3 -> x0, waiting for transfers between devices: 53.5 us -> none  [the longest x1 45.9 us: columns_body(): lax.all_to_all(jnp.stack([into, outof])[None], 'pipe', split_axis=3, conc...]
    dot_general x45 -> x0, matrix products: 42.4 us -> none  [the longest x16 18.4 us: trail(): lax.dot_general(left, right, (((1,), (1,)), ((), ())), preferred_element_...]
    all_to_all x2 -> x0, local copies, waits for them, and re-layouts: 20.5 us -> none  [the longest x1 10.3 us: columns_body(): lax.all_to_all(jnp.stack([into, outof])[None], 'pipe', split_axis=3, conc...]
    all_to_all x3 -> x0, starting transfers between devices: 13.9 us -> none  [the longest x1 5.29 us: columns_body(): lax.all_to_all(jnp.stack([inputs, cotangent], axis=1), 'pipe', split_axis...]
    unnamed x74 -> x28, local copies, waits for them, and re-layouts: 13.6 us -> 2.89 us
    another operation x3 -> x0, local copies, waits for them, and re-layouts: 8.31 us -> none  [the longest x1 6.77 us: columns_body(): jnp.stack([inputs, cotangent], axis=1)]
  transfers between devices with their start and end apart: 11 -> 0, of which waited for: 10 -> 0; matrix products, arithmetic and copies ran while one was open for 8% -> 0% of each run, Pallas kernels for 0% -> 0%
where the time goes in v2:
time: 88.4 us; the launch traced here: 88.2 us
  Pallas kernels  80.5 us (91%)
  other arithmetic  3.78 us (4%)
  local copies, waits for them, and re-layouts  3.06 us (3%)
    pallas_call x1, Pallas kernels, kernel_body(): pl.pallas_call(functools.partial(columns_kernel, (sections, members)), ou...  80.5 us
    unnamed x3, other arithmetic  3.4 us
    unnamed x28, local copies, waits for them, and re-layouts  2.89 us

profile of v2, /device:TPU:0, one launch (start us, length us, event | category | flops | bytes accessed | tf_op | source)
XLA Modules:
  0.0 88.2 jit_solution(2574621848944775789)
XLA Ops:
  0.6 0.0 copy-start.1
  0.6 0.0 copy-start.2
  0.7 0.0 copy-start.7
  0.7 0.0 copy-start.8
  0.7 0.0 copy-start.9
  0.7 0.0 copy-start.3
  0.7 0.0 copy-start.4
  0.7 1.3 %fusion.2 = bf16[160,8192]{1,0:T(8,128)(2,1)S(1)} fusion(f32[8192]{0:T(1024)} %bitcast.30, bf16[1,64,8192]{2,1,0:T(8,128)(2,1)} %param.15), kind=kLoop, calls=%fused_computation.4 | loop fusion | flops 786431 | bytes 1081344
  2.0 0.0 copy-start.6
  2.0 0.0 copy-start.5
  2.0 0.0 copy-start
  2.0 1.0 %fusion.5 = bf16[160,8192]{1,0:T(8,128)(2,1)S(1)} fusion(bf16[160,8192]{1,0:T(8,128)(2,1)S(1)} %fusion.2, bf16[1,1,16,8192]{3,2,1,0:T(8,128)(2,1)} %param.17, f32[8192]{0:T(1024)} %bitcast.31), kind=kLoop, calls=%fused_computation.10 | loop fusion | flops 393216 | bytes 557056
  3.0 1.1 %fusion.3 = bf16[160,8192]{1,0:T(8,128)(2,1)S(1)} fusion(bf16[160,8192]{1,0:T(8,128)(2,1)S(1)} %fusion.5, bf16[1,64,8192]{2,1,0:T(8,128)(2,1)} %param.15, f32[8192]{0:T(1024)} %bitcast.32), kind=kLoop, calls=%fused_computation.5 | loop fusion | flops 786432 | bytes 1081344
  4.2 0.0 copy-done.1
  4.2 0.0 copy-done.2
  4.3 0.0 copy-done.7
  4.3 0.0 copy-done.8
  4.3 0.0 copy-done.9
  4.3 0.2 select_reduce_fusion.1
  4.5 0.1 select_divide_fusion
  4.6 0.1 div.21.row_weight
  4.7 0.0 copy-done.3
  4.8 0.0 copy-done.4
  4.8 0.0 copy-done.6
  4.8 0.1 copy.28
  4.9 0.1 copy.29
  5.0 0.1 fusion.13.fac
  5.1 80.5 %shard_map.147 = (bf16[16,8192]{1,0:T(8,128)(2,1)S(1)}, bf16[16,64]{1,0:T(8,128)(2,1)S(1)}, bf16[16,64]{1,0:T(8,128)(2,1)S(1)}, bf16[16,8192]{1,0:T(8,128)(2,1)S(1)}) custom-call(bf16[16,8192]{1,0:T(8,128)(2,1)S(1)} %pad_maximum_fusion.tok, bf16[160,8192]{1,0:T(8,128)(2,1)S(1)} %bitcast_dynamic-update-slice_fusion.wts, bf16[80,128]{1,0:T(8,128)(2,1)S(1)} %fusion.13.fac, ...), custom_call_target="tpu_custom_call" | custom-call | tf_op jit(solution)/shard_map/pallas_call | solution.py:806
  85.6 0.7 copy.45
  86.3 0.6 copy.46
  86.9 0.6 copy.47
  87.5 0.7 copy.48
  (8 shorter events, 0.1 us)
Async XLA Ops:
  0.6 3.5 %copy-start.1 = (bf16[1,64,8192]{2,1,0:T(8,128)(2,1)S(1)}, bf16[1,64,8192]{2,1,0:T(8,128)(2,1)}, u32[]{:S(2)}) copy-start(bf16[1,64,8192]{2,1,0:T(8,128)(2,1)} %param.16) | copy-start | bytes 3145732
  0.6 3.6 %copy-start.2 = (bf16[1,1,16,8192]{3,2,1,0:T(8,128)(2,1)S(1)}, bf16[1,1,16,8192]{3,2,1,0:T(8,128)(2,1)}, u32[]{:S(2)}) copy-start(bf16[1,1,16,8192]{3,2,1,0:T(8,128)(2,1)} %param.20) | copy-start | bytes 786436
  0.7 3.6 %copy-start.7 = (s32[8]{0:T(128)S(1)}, s32[8]{0:T(128)}, u32[]{:S(2)}) copy-start(s32[8]{0:T(128)} %param.21) | copy-start | bytes 100
  0.7 3.6 %copy-start.8 = (s32[8]{0:T(128)S(1)}, s32[8]{0:T(128)}, u32[]{:S(2)}) copy-start(s32[8]{0:T(128)} %param.22) | copy-start | bytes 100
  0.7 3.6 %copy-start.9 = (s32[8]{0:T(128)S(1)}, s32[8]{0:T(128)}, u32[]{:S(2)}) copy-start(s32[8]{0:T(128)} %param.23) | copy-start | bytes 100
  0.7 4.1 %copy-start.3 = (bf16[1,8,8192]{2,1,0:T(8,128)(2,1)S(1)}, bf16[1,8,8192]{2,1,0:T(8,128)(2,1)}, u32[]{:S(2)}) copy-start(bf16[1,8,8192]{2,1,0:T(8,128)(2,1)} %param.13) | copy-start | bytes 393220
  0.7 4.1 %copy-start.4 = (bf16[1,8,8192]{2,1,0:T(8,128)(2,1)S(1)}, bf16[1,8,8192]{2,1,0:T(8,128)(2,1)}, u32[]{:S(2)}) copy-start(bf16[1,8,8192]{2,1,0:T(8,128)(2,1)} %param.12) | copy-start | bytes 393220
  2.0 2.8 %copy-start.6 = (bf16[1,1,16,64]{3,2,1,0:T(8,128)(2,1)S(1)}, bf16[1,1,16,64]{3,2,1,0:T(8,128)(2,1)}, u32[]{:S(2)}) copy-start(bf16[1,1,16,64]{3,2,1,0:T(8,128)(2,1)} %param.18) | copy-start | bytes 6148
  2.0 2.9 %copy-start.5 = (bf16[1,1,16,64]{3,2,1,0:T(8,128)(2,1)S(1)}, bf16[1,1,16,64]{3,2,1,0:T(8,128)(2,1)}, u32[]{:S(2)}) copy-start(bf16[1,1,16,64]{3,2,1,0:T(8,128)(2,1)} %param.19) | copy-start | bytes 6148
  2.0 3.1 %copy-start = (f32[1,8192]{1,0:T(1,128)S(1)}, f32[1,8192]{1,0:T(1,128)}, u32[]{:S(2)}) copy-start(f32[1,8192]{1,0:T(1,128)} %gain.1) | copy-start | bytes 98308

commit v3 on v2

--- a/solution.py
+++ b/solution.py
@@ -311,7 +311,11 @@
 def columns_kernel(
     shape,
     tok,
-    wts,
+    w_into,
+    a_into,
+    w_outof,
+    a_outof,
+    gain_row,
     fac,
     row_weight,
     gain,
@@ -323,9 +327,11 @@
     grad,
     cot,
     tbuf,
+    praw,
     pbuf,
     qbuf,
     fbuf,
+    gbuf,
     turned,
     land,
     mine,
@@ -336,8 +342,11 @@
     local_sem,
     tok_sem,
     fac_sem,
+    gain_sem,
     p_sem,
+    pa_sem,
     q_sem,
+    qa_sem,
     psib_sem,
     qsib_sem,
     x_up,
@@ -358,8 +367,14 @@
     row_total, columns = hid.shape[1:]
     block = row_total // members
     width = columns * sections
-    hd, rank = wts.shape[0] // 2 - out_vu.shape[0], out_vu.shape[0]
-    half, ranks = hd // 2, wts.shape[0] // 2
+    rank, hd = out_vu.shape
+    half, ranks = hd // 2, hd + rank
+    row_half = row_total // 2
+    near = lax.div(level, levels // 2) * row_half
+    half_rows = [
+        pl.ds(pl.multiple_of(near, row_half), row_half),
+        pl.ds(pl.multiple_of(row_half - near, row_half), row_half),
+    ]
     peers = [lax.rem(section + j, sections) for j in range(1, sections)]
     step = min(512, columns)
     chunks = columns // step
@@ -386,20 +401,25 @@
         pltpu.make_async_copy(tok.at[:, own_columns], tbuf.at[section], local_sem.at[0]),
         pltpu.make_async_copy(fac, fbuf.at[section], local_sem.at[1]),
         pltpu.make_async_copy(
-            wts.at[pl.ds(0, ranks), own_columns], pbuf.at[section], local_sem.at[2]
+            w_into.at[:, own_columns], praw.at[section, pl.ds(0, hd)], local_sem.at[2]
         ),
         pltpu.make_async_copy(
-            wts.at[pl.ds(ranks, ranks), own_columns], qbuf.at[section], local_sem.at[3]
+            a_into.at[:, own_columns], praw.at[section, pl.ds(hd, rank)], local_sem.at[3]
         ),
+        pltpu.make_async_copy(
+            w_outof.at[:, own_columns], qbuf.at[section, pl.ds(0, hd)], local_sem.at[4]
+        ),
+        pltpu.make_async_copy(
+            a_outof.at[:, own_columns], qbuf.at[section, pl.ds(hd, rank)], local_sem.at[5]
+        ),
+        pltpu.make_async_copy(gain_row.at[:, own_columns], gbuf.at[section], local_sem.at[6]),
     ]
     for copy in local:
         copy.start()
     pl.semaphore_wait(barrier, len(greeted))
 
-    share = half + rank
-    share_rows = pl.ds(pl.multiple_of(core * half, 16), share)
-    out_rows = pl.ds(pl.multiple_of(ranks + core * half, 16), share)
-    pass_rows = pl.ds(pl.multiple_of(core * share, 16), half)
+    share_rows = pl.ds(pl.multiple_of(core * half, half), half)
+    rank_rows = pl.ds(hd, rank)
 
     def to_columns(q):
         return pl.ds(pl.multiple_of(q * columns, columns), columns)
@@ -413,30 +433,50 @@
     def fac_copy(j, src_section):
         return remote(fac, fbuf.at[src_section], fac_sem, j, (peers[j], member), src_section)
 
-    def p_copy(j, src_section):
+    def gain_copy(j, src_section):
         q = peers[j]
         return remote(
-            wts.at[share_rows, to_columns(q)],
-            pbuf.at[src_section, share_rows],
-            p_sem,
+            gain_row.at[:, to_columns(q)],
+            gbuf.at[src_section],
+            gain_sem,
             j,
             (q, member),
             src_section,
         )
 
-    def q_copy(j, src_section):
-        q = peers[j]
-        return remote(
-            wts.at[out_rows, to_columns(q)],
-            qbuf.at[src_section, share_rows],
-            q_sem,
-            j,
-            (q, member),
-            src_section,
-        )
+    def weight_copy(src, buf, sem):
+        def copy_of(j, src_section):
+            q = peers[j]
+            return remote(
+                src.at[share_rows, to_columns(q)],
+                buf.at[src_section, share_rows],
+                sem,
+                j,
+                (q, member),
+                src_section,
+            )
+
+        return copy_of
+
+    def adapter_copy(src, buf, sem):
+        def copy_of(j, src_section):
+            q = peers[j]
+            return remote(
+                src.at[:, to_columns(q)],
+                buf.at[src_section, rank_rows],
+                sem,
+                j,
+                (q, member),
+                src_section,
+            )
+
+        return copy_of
+
+    p_copy, pa_copy = weight_copy(w_into, praw, p_sem), adapter_copy(a_into, praw, pa_sem)
+    q_copy, qa_copy = weight_copy(w_outof, qbuf, q_sem), adapter_copy(a_outof, qbuf, qa_sem)
 
     def sib_weight(buf, sem, layer):
-        piece = buf.at[layer, pass_rows]
+        piece = buf.at[layer, share_rows]
         return remote(piece, piece, sem, layer, sibling)
 
     def arrive(copy_of, layer):
@@ -514,32 +554,33 @@
         for at_level in range(levels):
             sib_copy(buf, sib, at_level).wait_send()
 
-    def sum_copy(out, into, sem, layer, j):
+    def sum_copy(out, into, sem, layer, part, j):
         return remote(
-            out.at[layer],
-            into.at[layer, j],
+            out.at[layer, part],
+            into.at[layer, part, j],
             sem,
-            layer * (sections - 1) + j,
+            (layer * 2 + part) * (sections - 1) + j,
             (peers[j], member),
         )
 
-    def send_sum(out, into, sem, layer, partial):
-        out[layer] = partial.astype(jnp.bfloat16)
+    def send_sum(out, into, sem, layer, part, partial):
+        out[layer, part] = partial.astype(jnp.bfloat16)
         for j in range(sections - 1):
-            sum_copy(out, into, sem, layer, j).start()
-
-    def whole_sum(out, into, sem, layer, partial):
+            sum_copy(out, into, sem, layer, part, j).start()
+
+    def whole_sum(out, into, sem, layer, part, partial):
         for j in range(sections - 1):
-            sum_copy(out, into, sem, layer, j).wait_recv()
+            sum_copy(out, into, sem, layer, part, j).wait_recv()
         for j in range(sections - 1):
-            partial = partial + into[layer, j].astype(jnp.float32)
+            partial = partial + into[layer, part, j].astype(jnp.float32)
         return partial
 
     for j in range(sections - 1):
         tok_copy(j, section).start()
     for j in range(sections - 1):
         p_copy(j, section).start()
-    for j in range(sections - 1):
+        pa_copy(j, section).start()
+        gain_copy(j, section).start()
         fac_copy(j, section).start()
 
     local[0].wait()
@@ -557,198 +598,268 @@
     sib_copy(x0, x_sib, level).start()
     for j in range(sections - 1):
         q_copy(j, section).start()
-    for k in range(levels - 1):
+        qa_copy(j, section).start()
+    for copy in local[1:]:
+        copy.wait()
+
+    ones = jnp.ones((16, 128), jnp.bfloat16)
+
+    def chunk(t):
+        return pl.ds(pl.multiple_of(t * step, step), step)
+
+    def project(layer, at, wide, rows):
+        squares = wide * wide
+        lanes = squares[:, :128]
+        for start in range(128, step, 128):
+            lanes = lanes + squares[:, start : start + 128]
+        return trail(pbuf[layer, :, at], rows), lanes
+
+    def add(left, right):
+        return tuple(a + b for a, b in zip(left, right))
+
+    zero_back = jnp.zeros((ranks, row_half), jnp.float32)
+    zero_sum = (zero_back, jnp.zeros((row_half, 128), jnp.float32))
+
+    def send_forward(layer, part, total):
+        lanes = total[1]
+        high = lanes.astype(jnp.bfloat16)
+        low = (lanes - high.astype(jnp.float32)).astype(jnp.bfloat16)
+        squares = (trail(ones, high) + trail(ones, low))[:8]
+        high = squares.astype(jnp.bfloat16).astype(jnp.float32)
+        partial = jnp.concatenate([total[0], high, squares - high])
+        send_sum(fx_out, fx_in, fx_sem, layer, part, partial)
+        return partial
+
+    def turn(parts):
+        parts = jnp.concatenate(parts)
+        spare = jnp.zeros((128 - parts.shape[0], row_half), jnp.float32)
+        return jnp.concatenate([parts, spare]).T
+
+    def in_order(parts):
+        wide = [part.astype(jnp.float32) for part in parts]
+        straight, swapped = jnp.concatenate(wide, axis=1), jnp.concatenate(wide[::-1], axis=1)
+        return jnp.where(near == 0, straight, swapped).astype(jnp.bfloat16)
+
+    def fold(layer):
+        passed(praw, psib_sem, layer)
+        pbuf[layer] = (praw[layer].astype(jnp.float32) * gbuf[layer]).astype(jnp.bfloat16)
+
+    def take_first(part):
+        def first(t, total):
+            rows = hid[0, half_rows[part], chunk(t)]
+            return add(total, project(0, chunk(t), rows.astype(jnp.float32), rows))
+
+        return send_forward(0, part, lax.fori_loop(0, chunks, first, zero_sum, unroll=True))
+
+    def line_levels(buf, sib, wanted):
+        for at_level in range(levels):
+
+            @pl.when((lax.div(at_level, levels // 2) == lax.div(level, levels // 2)) == wanted)
+            def _(at_level=at_level):
+                sib_copy(buf, sib, at_level).wait_recv()
+
+    reach = levels // 2 - 1
+    for k in range(reach):
+        line_arrive(x0, x_up, x_down, x_sib, k)
+    for layer in range(sections):
+        arrive_and_pass(p_copy, praw, psib_sem, layer)
+        arrive(pa_copy, layer)
+        arrive(gain_copy, layer)
+        arrive(fac_copy, layer)
+    fold(0)
+    line_levels(x0, x_sib, True)
+    partials = [take_first(0)]
+    for k in range(reach, levels - 1):
         line_arrive(x0, x_up, x_down, x_sib, k)
     line_start(cot, c_up, c_down, 0)
     sib_copy(cot, c_sib, level).start()
-    for copy in local[1:]:
-        copy.wait()
+    line_levels(x0, x_sib, False)
+    partials.append(take_first(1))
+
+    last = sections - 1
+    kept, sides, backs = [], [], [None, None]
     for layer in range(sections):
-        arrive_and_pass(p_copy, pbuf, psib_sem, layer)
-        arrive(fac_copy, layer)
-    for at_level in range(levels):
-        sib_copy(x0, x_sib, at_level).wait_recv()
-
-    ones = jnp.ones((16, step), jnp.bfloat16)
-
-    def chunk(t):
-        return pl.ds(pl.multiple_of(t * step, step), step)
-
-    def project(layer, at, rows):
-        squares = (rows.astype(jnp.float32) * rows.astype(jnp.float32)).astype(jnp.bfloat16)
-        return trail(pbuf[layer, :, at], rows), trail(ones, squares)
-
-    def add(left, right):
-        return tuple(a + b for a, b in zip(left, right))
-
-    zero_sum = (
-        jnp.zeros((ranks, row_total), jnp.float32),
-        jnp.zeros((16, row_total), jnp.float32),
-    )
-
-    def turn(parts):
-        parts = jnp.concatenate(parts)
-        spare = jnp.zeros((128 - parts.shape[0], row_total), jnp.float32)
-        return jnp.concatenate([parts, spare]).T
-
-    def first(t, total):
-        return add(total, project(0, chunk(t), hid[0, :, chunk(t)]))
-
-    passed(pbuf, psib_sem, 0)
-    total = lax.fori_loop(0, chunks, first, zero_sum)
-    kept = []
-    last = sections - 1
-    back = None
-    for layer in range(sections):
-        squares = total[1][:8]
-        high = squares.astype(jnp.bfloat16).astype(jnp.float32)
-        partial = jnp.concatenate([total[0], high, squares - high])
-        send_sum(fx_out, fx_in, fx_sem, layer, partial)
-        if layer < levels - 1:
-            line_arrive(cot, c_up, c_down, c_sib, layer)
+        if layer < last:
+            fold(layer + 1)
         if layer == 0:
             arrive_and_pass(q_copy, qbuf, qsib_sem, 0)
-            passed(qbuf, qsib_sem, 0)
+            arrive(qa_copy, 0)
         if layer == 1:
             for later in range(1, sections):
                 arrive_and_pass(q_copy, qbuf, qsib_sem, later)
-        if 0 < layer:
-            passed(qbuf, qsib_sem, layer)
-        if layer < last:
-            passed(pbuf, psib_sem, layer + 1)
+                arrive(qa_copy, later)
+        if layer < levels - 1:
+            line_arrive(cot, c_up, c_down, c_sib, layer)
+        passed(qbuf, qsib_sem, layer)
         if layer == last:
             for k in range(last + 1, levels - 1):
                 line_arrive(cot, c_up, c_down, c_sib, k)
             for at_level in range(levels):
                 sib_copy(cot, c_sib, at_level).wait_recv()
-
-            def seed(t, total_now):
-                at = chunk(t)
-                top = (cot[:, at].astype(jnp.float32) * row_weight[...]).astype(jnp.bfloat16)
-                grad[last, :, at] = top
-                return total_now + trail(qbuf[last, :, at], top)
-
-            back = lax.fori_loop(0, chunks, seed, zero_sum[0])
-            send_sum(bx_out, bx_in, bx_sem, last, back)
-        whole = whole_sum(fx_out, fx_in, fx_sem, layer, partial)
-        projection = whole[:ranks]
-        inverse = lax.rsqrt((whole[ranks : ranks + 1] + whole[ranks + 8 : ranks + 9]) / width + norm_eps)
+            for part in range(2):
+                rows_of = half_rows[part]
+
+                def seed(t, total_now, rows_of=rows_of):
+                    at = chunk(t)
+                    top = cot[rows_of, at].astype(jnp.float32) * row_weight[rows_of, :]
+                    top = top.astype(jnp.bfloat16)
+                    grad[last, rows_of, at] = top
+                    return total_now + trail(qbuf[last, :, at], top)
+
+                backs[part] = lax.fori_loop(0, chunks, seed, zero_back, unroll=True)
+                send_sum(bx_out, bx_in, bx_sem, last, part, backs[part])
         factor = fbuf[layer]
-        scaled = projection * inverse
-        lowrank = scaled[half : half + rank].astype(jnp.bfloat16)
-        straight = jnp.concatenate([scaled[:half], scaled[half + rank :]])
-        value = (
-            straight + adapter_scale * plain(factor[rank:, :rank], lowrank)
-        ).astype(jnp.bfloat16)
-        side = plain(factor[:rank, hd : 2 * hd], value).astype(jnp.bfloat16)
-        kept.append((projection, inverse, lowrank, value, side))
-        if layer < last:
-            wide_value = value.astype(jnp.float32)
-            mixed = [
-                wide_value[:half],
-                adapter_scale * side.astype(jnp.float32),
-                wide_value[half:],
-            ]
-            turned[...] = turn(mixed).astype(jnp.bfloat16)
-
-            def update(t, total_now, layer=layer):
-                at = chunk(t)
-                rows = hid[layer, :, at].astype(jnp.float32)
-                rows = rows + plain(turned[:, :ranks], qbuf[layer, :, at])
-                rows = rows.astype(jnp.bfloat16)
-                hid[layer + 1, :, at] = rows
-                return add(total_now, project(layer + 1, at, rows))
-
-            total = lax.fori_loop(0, chunks, update, zero_sum)
-
+        halves = []
+        for part in range(2):
+            rows_of = half_rows[part]
+            whole = whole_sum(fx_out, fx_in, fx_sem, layer, part, partials[part])
+            projection = whole[:ranks]
+            squares = whole[ranks : ranks + 1] + whole[ranks + 8 : ranks + 9]
+            inverse = lax.rsqrt(squares / width + norm_eps)
+            scaled = projection * inverse
+            lowrank = scaled[hd:].astype(jnp.bfloat16)
+            value = (
+                scaled[:hd] + adapter_scale * plain(factor[rank:, :rank], lowrank)
+            ).astype(jnp.bfloat16)
+            side = plain(factor[:rank, hd : 2 * hd], value).astype(jnp.bfloat16)
+            halves.append((projection, inverse, lowrank, value, side))
+            if layer < last:
+                mixed = [value.astype(jnp.float32), adapter_scale * side.astype(jnp.float32)]
+                turned[part] = turn(mixed).astype(jnp.bfloat16)
+
+                def update(t, total_now, layer=layer, part=part, rows_of=rows_of):
+                    at = chunk(t)
+                    rows = hid[layer, rows_of, at].astype(jnp.float32)
+                    rows = rows + plain(turned[part, :, :ranks], qbuf[layer, :, at])
+                    rows = rows.astype(jnp.bfloat16)
+                    hid[layer + 1, rows_of, at] = rows
+                    return add(
+                        total_now, project(layer + 1, at, rows.astype(jnp.float32), rows)
+                    )
+
+                total = lax.fori_loop(0, chunks, update, zero_sum, unroll=True)
+                partials[part] = send_forward(layer + 1, part, total)
+        kept.append(halves)
+        sides.append(in_order([h[4] for h in halves]))
+
+    def land_copy(layer, which):
+        return remote(
+            mine.at[layer, which],
+            land.at[section, which],
+            land_sem,
+            layer * 2 + which,
+            (layer, member),
+            section * 2 + which,
+        )
+
+    def collect(layer, which, small, wide, by):
+        def gather(t, carry):
+            at = chunk(t)
+            mine[layer, which, :, at] = (by * plain(small, wide[layer, :, at])).astype(
+                jnp.bfloat16
+            )
+            return carry
+
+        lax.fori_loop(0, chunks, gather, 0, unroll=True)
+
+        @pl.when(section != layer)
+        def _():
+            land_copy(layer, which).start()
+
+        @pl.when(section == layer)
+        def _():
+            land[layer, which] = mine[layer, which]
+
+    collect(last, 1, sides[last], grad, adapter_scale)
     for layer in reversed(range(sections)):
-        projection, inverse, lowrank, value, side = kept[layer]
         factor = fbuf[layer]
-        whole = whole_sum(bx_out, bx_in, bx_sem, layer, back)
-        grad_side = (adapter_scale * whole[half : half + rank]).astype(jnp.bfloat16)
-        straight = jnp.concatenate([whole[:half], whole[half + rank :]])
-        grad_value = (straight + plain(factor[rank:, hd : hd + rank], grad_side)).astype(
-            jnp.bfloat16
-        )
-        grad_low = (adapter_scale * plain(factor[:rank, :hd], grad_value)).astype(jnp.bfloat16)
-        wide_value = grad_value.astype(jnp.float32)
-        both = jnp.concatenate(
-            [wide_value[:half], grad_low.astype(jnp.float32), wide_value[half:]]
-        )
-        scaled = both * inverse
+        lows, small_up, small_down = [], None, None
+        for part in range(2):
+            rows_of = half_rows[part]
+            projection, inverse, lowrank, value, side = kept[layer][part]
+            whole = whole_sum(bx_out, bx_in, bx_sem, layer, part, backs[part])
+            grad_side = (adapter_scale * whole[hd:]).astype(jnp.bfloat16)
+            grad_value = (whole[:hd] + plain(factor[rank:, hd : hd + rank], grad_side)).astype(
+                jnp.bfloat16
+            )
+            grad_low = (adapter_scale * plain(factor[:rank, :hd], grad_value)).astype(
+                jnp.bfloat16
+            )
+            both = jnp.concatenate(
+                [grad_value.astype(jnp.float32), grad_low.astype(jnp.float32)]
+            )
+            scaled = both * inverse
+            lows.append(scaled[hd:])
+            if layer > 0:
+                correction = jnp.sum(both * projection, axis=0, keepdims=True) / width
+                shrink = inverse * inverse * inverse * correction
+                shrink = jnp.broadcast_to(shrink, (8, row_half))
+                columns_of = turn([scaled, shrink])
+                turned[part] = columns_of.astype(jnp.bfloat16)
+                shrink_column = columns_of[:, ranks : ranks + 1]
+
+                def step_back(
+                    t, total_now, layer=layer, part=part, rows_of=rows_of, shrink=shrink_column
+                ):
+                    at = chunk(t)
+                    rows = hid[layer, rows_of, at].astype(jnp.float32)
+                    fresh = grad[layer, rows_of, at].astype(jnp.float32)
+                    fresh = fresh + plain(turned[part, :, :ranks], pbuf[layer, :, at])
+                    fresh = (fresh - rows * shrink).astype(jnp.bfloat16)
+                    grad[layer - 1, rows_of, at] = fresh
+                    return total_now + trail(qbuf[layer - 1, :, at], fresh)
+
+                backs[part] = lax.fori_loop(0, chunks, step_back, zero_back, unroll=True)
+                send_sum(bx_out, bx_in, bx_sem, layer - 1, part, backs[part])
+            up_now = trail(lowrank, grad_value)
+            down_now = trail(grad_side, value)
+            small_up = up_now if small_up is None else small_up + up_now
+            small_down = down_now if small_down is None else small_down + down_now
+        collect(layer, 0, in_order(lows), hid, 1.0)
         if layer > 0:
-            correction = jnp.sum(both * projection, axis=0, keepdims=True) / width
-            shrink = inverse * inverse * inverse * correction
-            shrink = jnp.broadcast_to(shrink, (8, row_total))
-            columns_of = turn([scaled, shrink])
-            turned[...] = columns_of.astype(jnp.bfloat16)
-            shrink_column = columns_of[:, ranks : ranks + 1]
-
-            def step_back(t, total_now, layer=layer, shrink_column=shrink_column):
-                at = chunk(t)
-                rows = hid[layer, :, at].astype(jnp.float32)
-                fresh = grad[layer, :, at].astype(jnp.float32)
-                fresh = fresh + plain(turned[:, :ranks], pbuf[layer, :, at])
-                fresh = (fresh - rows * shrink_column).astype(jnp.bfloat16)
-                grad[layer - 1, :, at] = fresh
-                return total_now + trail(qbuf[layer - 1, :, at], fresh)
-
-            back = lax.fori_loop(0, chunks, step_back, zero_sum[0])
-            send_sum(bx_out, bx_in, bx_sem, layer - 1, back)
-        low_scaled = scaled[half : half + rank].astype(jnp.bfloat16)
-
-        def gather(t, carry, layer=layer, low_scaled=low_scaled, side=side):
-            at = chunk(t)
-            mine[layer, 0, :, at] = plain(low_scaled, hid[layer, :, at]).astype(jnp.bfloat16)
-            mine[layer, 1, :, at] = (
-                adapter_scale * plain(side, grad[layer, :, at])
-            ).astype(jnp.bfloat16)
-            return carry
-
-        lax.fori_loop(0, chunks, gather, 0)
-        land_copy = remote(
-            mine.at[layer], land.at[section], land_sem, layer, (layer, member), section
-        )
+            collect(layer - 1, 1, sides[layer - 1], grad, adapter_scale)
+
+        @pl.when(section == layer)
+        def _(small_up=small_up, small_down=small_down):
+            out_vu[...] = (adapter_scale * small_up).astype(jnp.bfloat16)
+            out_od[...] = small_down.astype(jnp.bfloat16)
+
+    def landed(source, which):
+        @pl.when(section != source)
+        def _():
+            remote(
+                mine.at[source, which],
+                land.at[source, which],
+                land_sem,
+                source * 2 + which,
+                (source, member),
+                source * 2 + which,
+            ).wait()
+
+    for q in range(sections):
+        landed(q, 1)
+        at = pl.ds(q * columns, columns)
+        out_ou[:, at] = land[q, 1]
+    for j in range(sections - 1):
+        for copy_of in (tok_copy, fac_copy, gain_copy, p_copy, pa_copy, q_copy, qa_copy):
+            copy_of(j, section).wait_send()
+        for layer in range(sections):
+            for part in range(2):
+                sum_copy(fx_out, fx_in, fx_sem, layer, part, j).wait_send()
+                sum_copy(bx_out, bx_in, bx_sem, layer, part, j).wait_send()
+    for layer in range(sections):
 
         @pl.when(section != layer)
-        def _(land_copy=land_copy):
-            land_copy.start()
-
-        @pl.when(section == layer)
-        def _(layer=layer, lowrank=lowrank, grad_value=grad_value, grad_side=grad_side, value=value):
-            land[layer] = mine[layer]
-            out_vu[...] = (adapter_scale * trail(lowrank, grad_value)).astype(jnp.bfloat16)
-            out_od[...] = trail(grad_side, value).astype(jnp.bfloat16)
-
-    for source in range(sections):
-
-        @pl.when(section != source)
-        def _(source=source):
-            remote(
-                mine.at[source], land.at[source], land_sem, source, (source, member), source
-            ).wait()
-
+        def _(layer=layer):
+            sib_weight(praw, psib_sem, layer).wait_send()
+            sib_weight(qbuf, qsib_sem, layer).wait_send()
+
+    line_sent(x0, x_up, x_down, x_sib)
+    line_sent(cot, c_up, c_down, c_sib)
     for q in range(sections):
+        landed(q, 0)
         at = pl.ds(q * columns, columns)
         out_vd[:, at] = (land[q, 0].astype(jnp.float32) * gain[:, at]).astype(jnp.bfloat16)
-        out_ou[:, at] = land[q, 1]
-    for j in range(sections - 1):
-        tok_copy(j, section).wait_send()
-        fac_copy(j, section).wait_send()
-        p_copy(j, section).wait_send()
-        q_copy(j, section).wait_send()
-        for layer in range(sections):
-            sum_copy(fx_out, fx_in, fx_sem, layer, j).wait_send()
-            sum_copy(bx_out, bx_in, bx_sem, layer, j).wait_send()
-    for layer in range(sections):
-
-        @pl.when(section != layer)
-        def _(layer=layer):
-            sib_weight(pbuf, psib_sem, layer).wait_send()
-            sib_weight(qbuf, qsib_sem, layer).wait_send()
-
-    line_sent(x0, x_up, x_down, x_sib)
-    line_sent(cot, c_up, c_down, c_sib)
 
 
 def kernel_body(
@@ -771,22 +882,7 @@
     micro_count = inputs.shape[0] * sections
     columns, row_total = width // sections, micro_count * row_count * members
     rank, hd = value_up_factor.shape[2:]
-    half, ranks = hd // 2, hd + rank
-    gain = norm_gain[0][None]
-
-    def folded(rows):
-        return (rows.astype(jnp.float32) * gain).astype(jnp.bfloat16)
-
-    wts = jnp.concatenate(
-        [
-            folded(w_value[0, :half]),
-            folded(value_down[0, 0]),
-            folded(w_value[0, half:]),
-            w_out[0, :half],
-            output_up_factor[0, 0],
-            w_out[0, half:],
-        ]
-    )
+    ranks, row_half = hd + rank, row_total // 2
     tok = jnp.concatenate([inputs[0], cotangent[0]])
     up, down = value_up_factor[0, 0], out_down[0, 0]
     pad = ((0, 0), (0, hd - rank))
@@ -811,7 +907,7 @@
             jax.ShapeDtypeStruct((rank, hd), half_type),
             jax.ShapeDtypeStruct((rank, width), half_type),
         ),
-        in_specs=[anywhere, anywhere, anywhere, vmem, vmem],
+        in_specs=[anywhere] * 7 + [vmem, vmem],
         out_specs=(vmem, vmem, vmem, vmem),
         scratch_shapes=[
             pltpu.VMEM((sections, row_total, columns), half_type),
@@ -820,15 +916,20 @@
             pltpu.VMEM((sections, 2 * row_count, columns), half_type),
             pltpu.VMEM((sections, ranks, columns), half_type),
             pltpu.VMEM((sections, ranks, columns), half_type),
+            pltpu.VMEM((sections, ranks, columns), half_type),
             pltpu.VMEM((sections,) + fac.shape, half_type),
-            pltpu.VMEM((row_total, 128), half_type),
+            pltpu.VMEM((sections, 1, columns), jnp.float32),
+            pltpu.VMEM((2, row_half, 128), half_type),
             pltpu.VMEM((sections, 2, rank, columns), half_type),
             pltpu.VMEM((sections, 2, rank, columns), half_type),
-            pltpu.VMEM((sections, ranks + 16, row_total), half_type),
-            pltpu.VMEM((sections, sections - 1, ranks + 16, row_total), half_type),
-            pltpu.VMEM((sections, ranks, row_total), half_type),
-            pltpu.VMEM((sections, sections - 1, ranks, row_total), half_type),
-            dma((4,)),
+            pltpu.VMEM((sections, 2, ranks + 16, row_half), half_type),
+            pltpu.VMEM((sections, 2, sections - 1, ranks + 16, row_half), half_type),
+            pltpu.VMEM((sections, 2, ranks, row_half), half_type),
+            pltpu.VMEM((sections, 2, sections - 1, ranks, row_half), half_type),
+            dma((7,)),
+            dma((2, sections)),
+            dma((2, sections)),
+            dma((2, sections)),
             dma((2, sections)),
             dma((2, sections)),
             dma((2, sections)),
@@ -841,14 +942,24 @@
             dma((2, levels)),
             dma((2, levels)),
             dma((2, levels)),
-            dma((2, sums)),
-            dma((2, sums)),
-            dma((2, sections)),
+            dma((2, 2 * sums)),
+            dma((2, 2 * sums)),
+            dma((2, 2 * sections)),
         ],
         compiler_params=pltpu.CompilerParams(
             collective_id=0, has_side_effects=True, vmem_limit_bytes=50 * 2**20
         ),
-    )(tok, wts, fac, weight, gain)
+    )(
+        tok,
+        w_value[0],
+        value_down[0, 0],
+        w_out[0],
+        output_up_factor[0, 0],
+        norm_gain,
+        fac,
+        weight,
+        norm_gain,
+    )
     return tuple(part[None, None] for part in outs)
 
 

time: 88.4 us -> 78.8 us (0.89)
  Pallas kernels: 80.5 us -> 70.4 us
  local copies, waits for them, and re-layouts: 3.06 us -> 6.11 us
  other arithmetic: 3.78 us -> 1.34 us
    pallas_call x1, Pallas kernels: 80.5 us -> 70.4 us  [kernel_body(): pl.pallas_call(functools.partial(columns_kernel, (sections, members)), ou...]
    unnamed x3 -> x0, other arithmetic: 3.4 us -> none
    unnamed x28, local copies, waits for them, and re-layouts: 2.89 us -> 5.97 us
    concatenate x1, other arithmetic: 0.02 us -> 0.98 us  [kernel_body(): tok = jnp.concatenate([inputs[0], cotangent[0]])]
where the time goes in v3:
time: 78.8 us; the launch traced here: 78.6 us
  Pallas kernels  70.4 us (89%)
  local copies, waits for them, and re-layouts  6.11 us (8%)
  other arithmetic  1.34 us (2%)
    pallas_call x1, Pallas kernels, kernel_body(): pl.pallas_call(functools.partial(columns_kernel, (sections, members)), ou...  70.4 us
    unnamed x28, local copies, waits for them, and re-layouts  5.97 us

profile of v3, /device:TPU:0, one launch (start us, length us, event | category | flops | bytes accessed | tf_op | source)
XLA Modules:
  0.0 78.6 jit_solution(11405496273608470088)
XLA Ops:
  0.6 0.0 copy-start.8
  0.6 0.0 copy-start.9
  0.7 0.0 copy-start.10
  0.7 0.0 copy-start.7
  0.7 0.0 copy-start.6
  0.7 0.0 copy-start.5
  0.7 0.6 copy-done.8
  1.3 0.0 copy-done.9
  1.3 0.0 copy-done.10
  1.3 0.2 select_reduce_fusion.1
  1.5 0.1 select_divide_fusion
  1.6 0.0 copy-done.7
  1.6 0.1 copy.28
  1.7 0.0 copy-done.6
  1.7 0.1 copy.29
  1.8 0.1 fusion.7.fac
  1.9 0.0 copy-start.4
  1.9 0.1 div.21.row_weight
  2.0 0.0 copy-done.5
  2.0 0.0 copy-start.2
  2.1 0.0 copy-start.3
  2.1 1.0 %pad_maximum_fusion.tok = bf16[16,8192]{1,0:T(8,128)(2,1)S(1)} fusion(bf16[8,8192]{1,0:T(8,128)(2,1)S(1)} %bitcast.26, bf16[8,8192]{1,0:T(8,128)(2,1)} %bitcast.27), kind=kLoop, calls=%fused_computation | loop fusion | flops 524288 | bytes 524288 | tf_op jit(solution)/shard_map/concatenate | solution.py:886
  3.1 0.0 copy-done.4
  3.1 0.0 copy-done.2
  3.1 0.1 copy-done.3
  3.1 1.2 %copy-done = bf16[1,64,8192]{2,1,0:T(8,128)(2,1)S(1)} copy-done((bf16[1,64,8192]{2,1,0:T(8,128)(2,1)S(1)}, bf16[1,64,8192]{2,1,0:T(8,128)(2,1)}, u32[]{:S(2)}) %copy-start) | copy-done | bytes 1048600
  4.4 1.2 %copy-done.1 = bf16[1,64,8192]{2,1,0:T(8,128)(2,1)S(1)} copy-done((bf16[1,64,8192]{2,1,0:T(8,128)(2,1)S(1)}, bf16[1,64,8192]{2,1,0:T(8,128)(2,1)}, u32[]{:S(2)}) %copy-start.1) | copy-done | bytes 1048600
  5.6 70.4 %shard_map.147 = (bf16[16,8192]{1,0:T(8,128)(2,1)S(1)}, bf16[16,64]{1,0:T(8,128)(2,1)S(1)}, bf16[16,64]{1,0:T(8,128)(2,1)S(1)}, bf16[16,8192]{1,0:T(8,128)(2,1)S(1)}) custom-call(bf16[16,8192]{1,0:T(8,128)(2,1)S(1)} %pad_maximum_fusion.tok, bf16[64,8192]{1,0:T(8,128)(2,1)S(1)} %bitcast.18, bf16[16,8192]{1,0:T(8,128)(2,1)S(1)} %bitcast.20, ...), custom_call_target="tpu_custom_call" | custom-call | tf_op jit(solution)/shard_map/pallas_call | solution.py:902
  76.0 0.7 copy.40
  76.7 0.6 copy.41
  77.3 0.6 copy.42
  77.9 0.7 copy.43
  (4 shorter events, 0.0 us)
Async XLA Ops:
  0.6 0.7 copy-start.8
  0.6 0.7 copy-start.9
  0.7 0.7 copy-start.10
  0.7 0.9 %copy-start.7 = (bf16[1,1,16,64]{3,2,1,0:T(8,128)(2,1)S(1)}, bf16[1,1,16,64]{3,2,1,0:T(8,128)(2,1)}, u32[]{:S(2)}) copy-start(bf16[1,1,16,64]{3,2,1,0:T(8,128)(2,1)} %param.18) | copy-start | bytes 6148
  0.7 1.0 %copy-start.6 = (bf16[1,1,16,64]{3,2,1,0:T(8,128)(2,1)S(1)}, bf16[1,1,16,64]{3,2,1,0:T(8,128)(2,1)}, u32[]{:S(2)}) copy-start(bf16[1,1,16,64]{3,2,1,0:T(8,128)(2,1)} %param.19) | copy-start | bytes 6148
  0.7 1.4 %copy-start.5 = (bf16[1,8,8192]{2,1,0:T(8,128)(2,1)S(1)}, bf16[1,8,8192]{2,1,0:T(8,128)(2,1)}, u32[]{:S(2)}) copy-start(bf16[1,8,8192]{2,1,0:T(8,128)(2,1)} %param.13) | copy-start | bytes 393220
  1.9 1.2 %copy-start.4 = (f32[1,8192]{1,0:T(1,128)S(1)}, f32[1,8192]{1,0:T(1,128)}, u32[]{:S(2)}) copy-start(f32[1,8192]{1,0:T(1,128)} %gain.1) | copy-start | bytes 98308
  2.0 1.0 %copy-start.2 = (bf16[1,1,16,8192]{3,2,1,0:T(8,128)(2,1)S(1)}, bf16[1,1,16,8192]{3,2,1,0:T(8,128)(2,1)}, u32[]{:S(2)}) copy-start(bf16[1,1,16,8192]{3,2,1,0:T(8,128)(2,1)} %param.17) | copy-start | bytes 786436
  2.1 1.1 %copy-start.3 = (bf16[1,1,16,8192]{3,2,1,0:T(8,128)(2,1)S(1)}, bf16[1,1,16,8192]{3,2,1,0:T(8,128)(2,1)}, u32[]{:S(2)}) copy-start(bf16[1,1,16,8192]{3,2,1,0:T(8,128)(2,1)} %param.20) | copy-start | bytes 786436
  3.1 1.2 %copy-start = (bf16[1,64,8192]{2,1,0:T(8,128)(2,1)S(1)}, bf16[1,64,8192]{2,1,0:T(8,128)(2,1)}, u32[]{:S(2)}) copy-start(bf16[1,64,8192]{2,1,0:T(8,128)(2,1)} %param.15) | copy-start | bytes 3145732
  4.4 1.2 %copy-start.1 = (bf16[1,64,8192]{2,1,0:T(8,128)(2,1)S(1)}, bf16[1,64,8192]{2,1,0:T(8,128)(2,1)}, u32[]{:S(2)}) copy-start(bf16[1,64,8192]{2,1,0:T(8,128)(2,1)} %param.16) | copy-start | bytes 3145732

commit v4 on v3

--- a/solution.py
+++ b/solution.py
@@ -330,6 +330,8 @@
     praw,
     pbuf,
     qbuf,
+    pfold,
+    qfold,
     fbuf,
     gbuf,
     turned,
@@ -644,6 +646,26 @@
         passed(praw, psib_sem, layer)
         pbuf[layer] = (praw[layer].astype(jnp.float32) * gbuf[layer]).astype(jnp.bfloat16)
 
+    def fold_rank(layer, raw, folded, top_by, low_by):
+        def piece(t, carry):
+            at = chunk(t)
+            top = raw[layer, :hd, at].astype(jnp.float32)
+            top = top + adapter_scale * plain(top_by, raw[layer, hd:, at])
+            top = top.astype(jnp.bfloat16)
+            folded[layer, :hd, at] = top
+            folded[layer, hd:, at] = (adapter_scale * plain(low_by, top)).astype(jnp.bfloat16)
+            return carry
+
+        lax.fori_loop(0, chunks, piece, 0)
+
+    def fold_into(layer):
+        factor = fbuf[layer]
+        fold_rank(layer, pbuf, pfold, factor[rank:, :rank], factor[:rank, hd : 2 * hd])
+
+    def fold_outof(layer):
+        factor = fbuf[layer]
+        fold_rank(layer, qbuf, qfold, factor[rank:, hd : hd + rank], factor[:rank, :hd])
+
     def take_first(part):
         def first(t, total):
             rows = hid[0, half_rows[part], chunk(t)]
@@ -679,9 +701,10 @@
     last = sections - 1
     kept, sides, backs = [], [], [None, None]
     for layer in range(sections):
-        if layer < last:
-            fold(layer + 1)
         if layer == 0:
+            for later in range(1, sections):
+                fold(later)
+                fold_into(later)
             arrive_and_pass(q_copy, qbuf, qsib_sem, 0)
             arrive(qa_copy, 0)
         if layer == 1:
@@ -691,6 +714,8 @@
         if layer < levels - 1:
             line_arrive(cot, c_up, c_down, c_sib, layer)
         passed(qbuf, qsib_sem, layer)
+        if layer < last:
+            fold_outof(layer)
         if layer == last:
             for k in range(last + 1, levels - 1):
                 line_arrive(cot, c_up, c_down, c_sib, k)
@@ -717,30 +742,35 @@
             squares = whole[ranks : ranks + 1] + whole[ranks + 8 : ranks + 9]
             inverse = lax.rsqrt(squares / width + norm_eps)
             scaled = projection * inverse
+            halves.append((scaled, inverse))
+            if layer < last:
+                turned[part] = turn([scaled]).astype(jnp.bfloat16)
+
+                def update(t, total_now, layer=layer, part=part, rows_of=rows_of):
+                    at = chunk(t)
+                    rows = hid[layer, rows_of, at].astype(jnp.float32)
+                    rows = rows + plain(turned[part, :, :ranks], qfold[layer, :, at])
+                    rows = rows.astype(jnp.bfloat16)
+                    hid[layer + 1, rows_of, at] = rows
+                    return add(
+                        total_now, project(layer + 1, at, rows.astype(jnp.float32), rows)
+                    )
+
+                total = lax.fori_loop(0, chunks, update, zero_sum, unroll=True)
+                partials[part] = send_forward(layer + 1, part, total)
+        smalls = []
+        for scaled, inverse in halves:
             lowrank = scaled[hd:].astype(jnp.bfloat16)
             value = (
                 scaled[:hd] + adapter_scale * plain(factor[rank:, :rank], lowrank)
             ).astype(jnp.bfloat16)
             side = plain(factor[:rank, hd : 2 * hd], value).astype(jnp.bfloat16)
-            halves.append((projection, inverse, lowrank, value, side))
-            if layer < last:
-                mixed = [value.astype(jnp.float32), adapter_scale * side.astype(jnp.float32)]
-                turned[part] = turn(mixed).astype(jnp.bfloat16)
-
-                def update(t, total_now, layer=layer, part=part, rows_of=rows_of):
-                    at = chunk(t)
-                    rows = hid[layer, rows_of, at].astype(jnp.float32)
-                    rows = rows + plain(turned[part, :, :ranks], qbuf[layer, :, at])
-                    rows = rows.astype(jnp.bfloat16)
-                    hid[layer + 1, rows_of, at] = rows
-                    return add(
-                        total_now, project(layer + 1, at, rows.astype(jnp.float32), rows)
-                    )
-
-                total = lax.fori_loop(0, chunks, update, zero_sum, unroll=True)
-                partials[part] = send_forward(layer + 1, part, total)
-        kept.append(halves)
-        sides.append(in_order([h[4] for h in halves]))
+            mixed = jnp.concatenate(
+                [value.astype(jnp.float32), adapter_scale * side.astype(jnp.float32)]
+            )
+            smalls.append((mixed, inverse, lowrank, value, side))
+        kept.append(smalls)
+        sides.append(in_order([h[4] for h in smalls]))
 
     def land_copy(layer, which):
         return remote(
@@ -774,10 +804,33 @@
     for layer in reversed(range(sections)):
         factor = fbuf[layer]
         lows, small_up, small_down = [], None, None
+        wholes = []
         for part in range(2):
             rows_of = half_rows[part]
-            projection, inverse, lowrank, value, side = kept[layer][part]
+            mixed, inverse = kept[layer][part][:2]
             whole = whole_sum(bx_out, bx_in, bx_sem, layer, part, backs[part])
+            wholes.append(whole)
+            if layer > 0:
+                correction = jnp.sum(whole * mixed, axis=0, keepdims=True) / width
+                shrink = jnp.broadcast_to(inverse * inverse * correction, (8, row_half))
+                columns_of = turn([whole * inverse, shrink])
+                turned[part] = columns_of.astype(jnp.bfloat16)
+                shrink_column = columns_of[:, ranks : ranks + 1]
+
+                def step_back(
+                    t, total_now, layer=layer, part=part, rows_of=rows_of, shrink=shrink_column
+                ):
+                    at = chunk(t)
+                    rows = hid[layer, rows_of, at].astype(jnp.float32)
+                    fresh = grad[layer, rows_of, at].astype(jnp.float32)
+                    fresh = fresh + plain(turned[part, :, :ranks], pfold[layer, :, at])
+                    fresh = (fresh - rows * shrink).astype(jnp.bfloat16)
+                    grad[layer - 1, rows_of, at] = fresh
+                    return total_now + trail(qbuf[layer - 1, :, at], fresh)
+
+                backs[part] = lax.fori_loop(0, chunks, step_back, zero_back, unroll=True)
+                send_sum(bx_out, bx_in, bx_sem, layer - 1, part, backs[part])
+        for whole, (mixed, inverse, lowrank, value, side) in zip(wholes, kept[layer]):
             grad_side = (adapter_scale * whole[hd:]).astype(jnp.bfloat16)
             grad_value = (whole[:hd] + plain(factor[rank:, hd : hd + rank], grad_side)).astype(
                 jnp.bfloat16
@@ -785,32 +838,7 @@
             grad_low = (adapter_scale * plain(factor[:rank, :hd], grad_value)).astype(
                 jnp.bfloat16
             )
-            both = jnp.concatenate(
-                [grad_value.astype(jnp.float32), grad_low.astype(jnp.float32)]
-            )
-            scaled = both * inverse
-            lows.append(scaled[hd:])
-            if layer > 0:
-                correction = jnp.sum(both * projection, axis=0, keepdims=True) / width
-                shrink = inverse * inverse * inverse * correction
-                shrink = jnp.broadcast_to(shrink, (8, row_half))
-                columns_of = turn([scaled, shrink])
-                turned[part] = columns_of.astype(jnp.bfloat16)
-                shrink_column = columns_of[:, ranks : ranks + 1]
-
-                def step_back(
-                    t, total_now, layer=layer, part=part, rows_of=rows_of, shrink=shrink_column
-                ):
-                    at = chunk(t)
-                    rows = hid[layer, rows_of, at].astype(jnp.float32)
-                    fresh = grad[layer, rows_of, at].astype(jnp.float32)
-                    fresh = fresh + plain(turned[part, :, :ranks], pbuf[layer, :, at])
-                    fresh = (fresh - rows * shrink).astype(jnp.bfloat16)
-                    grad[layer - 1, rows_of, at] = fresh
-                    return total_now + trail(qbuf[layer - 1, :, at], fresh)
-
-                backs[part] = lax.fori_loop(0, chunks, step_back, zero_back, unroll=True)
-                send_sum(bx_out, bx_in, bx_sem, layer - 1, part, backs[part])
+            lows.append(grad_low.astype(jnp.float32) * inverse)
             up_now = trail(lowrank, grad_value)
             down_now = trail(grad_side, value)
             small_up = up_now if small_up is None else small_up + up_now
@@ -914,6 +942,8 @@
             pltpu.VMEM((sections, row_total, columns), half_type),
             pltpu.VMEM((row_total, columns), half_type),
             pltpu.VMEM((sections, 2 * row_count, columns), half_type),
+            pltpu.VMEM((sections, ranks, columns), half_type),
+            pltpu.VMEM((sections, ranks, columns), half_type),
             pltpu.VMEM((sections, ranks, columns), half_type),
             pltpu.VMEM((sections, ranks, columns), half_type),
             pltpu.VMEM((sections, ranks, columns), half_type),
@@ -947,7 +977,7 @@
             dma((2, 2 * sections)),
         ],
         compiler_params=pltpu.CompilerParams(
-            collective_id=0, has_side_effects=True, vmem_limit_bytes=50 * 2**20
+            collective_id=0, has_side_effects=True, vmem_limit_bytes=60 * 2**20
         ),
     )(
         tok,

time: 78.8 us -> 82.2 us (1.043)
  Pallas kernels: 70.4 us -> 74.2 us
    pallas_call x1, Pallas kernels: 70.4 us -> 74.2 us  [kernel_body(): pl.pallas_call(functools.partial(columns_kernel, (sections, members)), ou...]
    unnamed x28 -> x26, local copies, waits for them, and re-layouts: 5.97 us -> 4.55 us
where the time goes in v4:
time: 82.2 us; the launch traced here: 82 us
  Pallas kernels  74.2 us (90%)
  local copies, waits for them, and re-layouts  5.34 us (6%)
  other arithmetic  1.67 us (2%)
    pallas_call x1, Pallas kernels, kernel_body(): pl.pallas_call(functools.partial(columns_kernel, (sections, members)), ou...  74.2 us
    unnamed x26, local copies, waits for them, and re-layouts  4.55 us

profile of v4, /device:TPU:0, one launch (start us, length us, event | category | flops | bytes accessed | tf_op | source)
XLA Modules:
  0.0 82.0 jit_solution(11508626218506225742)
XLA Ops:
  0.6 0.0 copy-start.9
  0.6 0.0 copy-start.4
  0.7 0.0 copy-start.3
  0.7 0.0 copy-start.7
  0.7 0.0 copy-start.8
  0.7 0.0 copy-start.2
  0.7 0.0 copy-start.1
  0.7 0.6 copy-done.9
  1.3 0.0 copy-done.7
  1.3 0.0 copy-done.8
  1.4 0.2 select_reduce_fusion.1
  1.6 0.1 select_divide_fusion
  1.6 0.0 copy-done.4
  1.6 0.1 copy.28
  1.7 0.0 copy-done.3
  1.7 0.1 copy.29
  1.8 0.7 fusion.7.fac
  2.5 0.8 div.21.row_weight
  3.3 0.0 copy-done.2
  3.3 0.0 copy-done.1
  3.3 0.7 pad_maximum_fusion.tok
  4.0 74.2 %shard_map.147 = (bf16[16,8192]{1,0:T(8,128)(2,1)}, bf16[16,64]{1,0:T(8,128)(2,1)}, bf16[16,64]{1,0:T(8,128)(2,1)}, bf16[16,8192]{1,0:T(8,128)(2,1)}) custom-call(bf16[16,8192]{1,0:T(8,128)(2,1)} %pad_maximum_fusion.tok, bf16[64,8192]{1,0:T(8,128)(2,1)} %bitcast.18, bf16[16,8192]{1,0:T(8,128)(2,1)} %bitcast.20, bf16[64,8192]{1,0:T(8,128)(2,1)} %bitcast.19, ...), custom_call_target="tpu_custom_call" | custom-call | tf_op jit(solution)/shard_map/pallas_call | solution.py:930
  78.3 0.0 copy-start.6
  78.3 0.0 copy-start
  78.3 1.7 %copy.40 = bf16[1,1,16,8192]{3,2,1,0:T(8,128)(2,1)} copy(bf16[1,1,16,8192]{3,2,1,0:T(8,128)(2,1)} %bitcast.23) | data formatting | bytes 524288
  80.0 0.0 copy-done.6
  80.0 0.0 copy-start.5
  80.0 0.6 copy.41
  80.6 0.1 copy-done.5
  80.7 0.6 copy.42
  81.3 0.0 copy-done
  81.3 0.7 copy.43
  (2 shorter events, 0.0 us)
Async XLA Ops:
  0.6 0.7 copy-start.9
  0.6 1.0 %copy-start.4 = (bf16[1,1,16,64]{3,2,1,0:T(8,128)(2,1)S(1)}, bf16[1,1,16,64]{3,2,1,0:T(8,128)(2,1)}, u32[]{:S(2)}) copy-start(bf16[1,1,16,64]{3,2,1,0:T(8,128)(2,1)} %param.18) | copy-start | bytes 6148
  0.7 1.1 %copy-start.3 = (bf16[1,1,16,64]{3,2,1,0:T(8,128)(2,1)S(1)}, bf16[1,1,16,64]{3,2,1,0:T(8,128)(2,1)}, u32[]{:S(2)}) copy-start(bf16[1,1,16,64]{3,2,1,0:T(8,128)(2,1)} %param.19) | copy-start | bytes 6148
  0.7 0.7 copy-start.7
  0.7 0.7 copy-start.8
  0.7 2.6 %copy-start.2 = (bf16[1,8,8192]{2,1,0:T(8,128)(2,1)S(1)}, bf16[1,8,8192]{2,1,0:T(8,128)(2,1)}, u32[]{:S(2)}) copy-start(bf16[1,8,8192]{2,1,0:T(8,128)(2,1)} %param.12) | copy-start | bytes 393220
  0.7 2.6 %copy-start.1 = (bf16[1,8,8192]{2,1,0:T(8,128)(2,1)S(1)}, bf16[1,8,8192]{2,1,0:T(8,128)(2,1)}, u32[]{:S(2)}) copy-start(bf16[1,8,8192]{2,1,0:T(8,128)(2,1)} %param.13) | copy-start | bytes 393220
  78.3 1.7 %copy-start.6 = (bf16[16,64]{1,0:T(8,128)(2,1)S(1)}, bf16[16,64]{1,0:T(8,128)(2,1)}, u32[]{:S(2)}) copy-start(bf16[16,64]{1,0:T(8,128)(2,1)} %get-tuple-element.9) | copy-start | bytes 6148
  78.3 3.0 %copy-start = (bf16[16,8192]{1,0:T(8,128)(2,1)S(1)}, bf16[16,8192]{1,0:T(8,128)(2,1)}, u32[]{:S(2)}) copy-start(bf16[16,8192]{1,0:T(8,128)(2,1)} %get-tuple-element.11) | copy-start | bytes 786436
  80.0 0.7 copy-start.5

commit v5 on v4

--- a/solution.py
+++ b/solution.py
@@ -331,7 +331,6 @@
     pbuf,
     qbuf,
     pfold,
-    qfold,
     fbuf,
     gbuf,
     turned,
@@ -662,10 +661,6 @@
         factor = fbuf[layer]
         fold_rank(layer, pbuf, pfold, factor[rank:, :rank], factor[:rank, hd : 2 * hd])
 
-    def fold_outof(layer):
-        factor = fbuf[layer]
-        fold_rank(layer, qbuf, qfold, factor[rank:, hd : hd + rank], factor[:rank, :hd])
-
     def take_first(part):
         def first(t, total):
             rows = hid[0, half_rows[part], chunk(t)]
@@ -714,8 +709,6 @@
         if layer < levels - 1:
             line_arrive(cot, c_up, c_down, c_sib, layer)
         passed(qbuf, qsib_sem, layer)
-        if layer < last:
-            fold_outof(layer)
         if layer == last:
             for k in range(last + 1, levels - 1):
                 line_arrive(cot, c_up, c_down, c_sib, k)
@@ -742,24 +735,6 @@
             squares = whole[ranks : ranks + 1] + whole[ranks + 8 : ranks + 9]
             inverse = lax.rsqrt(squares / width + norm_eps)
             scaled = projection * inverse
-            halves.append((scaled, inverse))
-            if layer < last:
-                turned[part] = turn([scaled]).astype(jnp.bfloat16)
-
-                def update(t, total_now, layer=layer, part=part, rows_of=rows_of):
-                    at = chunk(t)
-                    rows = hid[layer, rows_of, at].astype(jnp.float32)
-                    rows = rows + plain(turned[part, :, :ranks], qfold[layer, :, at])
-                    rows = rows.astype(jnp.bfloat16)
-                    hid[layer + 1, rows_of, at] = rows
-                    return add(
-                        total_now, project(layer + 1, at, rows.astype(jnp.float32), rows)
-                    )
-
-                total = lax.fori_loop(0, chunks, update, zero_sum, unroll=True)
-                partials[part] = send_forward(layer + 1, part, total)
-        smalls = []
-        for scaled, inverse in halves:
             lowrank = scaled[hd:].astype(jnp.bfloat16)
             value = (
                 scaled[:hd] + adapter_scale * plain(factor[rank:, :rank], lowrank)
@@ -768,9 +743,24 @@
             mixed = jnp.concatenate(
                 [value.astype(jnp.float32), adapter_scale * side.astype(jnp.float32)]
             )
-            smalls.append((mixed, inverse, lowrank, value, side))
-        kept.append(smalls)
-        sides.append(in_order([h[4] for h in smalls]))
+            halves.append((mixed, inverse, lowrank, value, side))
+            if layer < last:
+                turned[part] = turn([mixed]).astype(jnp.bfloat16)
+
+                def update(t, total_now, layer=layer, part=part, rows_of=rows_of):
+                    at = chunk(t)
+                    rows = hid[layer, rows_of, at].astype(jnp.float32)
+                    rows = rows + plain(turned[part, :, :ranks], qbuf[layer, :, at])
+                    rows = rows.astype(jnp.bfloat16)
+                    hid[layer + 1, rows_of, at] = rows
+                    return add(
+                        total_now, project(layer + 1, at, rows.astype(jnp.float32), rows)
+                    )
+
+                total = lax.fori_loop(0, chunks, update, zero_sum, unroll=True)
+                partials[part] = send_forward(layer + 1, part, total)
+        kept.append(halves)
+        sides.append(in_order([h[4] for h in halves]))
 
     def land_copy(layer, which):
         return remote(
@@ -942,7 +932,6 @@
             pltpu.VMEM((sections, row_total, columns), half_type),
             pltpu.VMEM((row_total, columns), half_type),
             pltpu.VMEM((sections, 2 * row_count, columns), half_type),
-            pltpu.VMEM((sections, ranks, columns), half_type),
             pltpu.VMEM((sections, ranks, columns), half_type),
             pltpu.VMEM((sections, ranks, columns), half_type),
             pltpu.VMEM((sections, ranks, columns), half_type),

time: 82.2 us -> 79.9 us (0.972)
  Pallas kernels: 74.2 us -> 71.9 us
    pallas_call x1, Pallas kernels: 74.2 us -> 71.9 us  [kernel_body(): pl.pallas_call(functools.partial(columns_kernel, (sections, members)), ou...]
where the time goes in v5:
time: 79.9 us; the launch traced here: 79.7 us
  Pallas kernels  71.9 us (90%)
  local copies, waits for them, and re-layouts  5.34 us (7%)
  other arithmetic  1.67 us (2%)
    pallas_call x1, Pallas kernels, kernel_body(): pl.pallas_call(functools.partial(columns_kernel, (sections, members)), ou...  71.9 us
    unnamed x26, local copies, waits for them, and re-layouts  4.55 us

profile of v5, /device:TPU:0, one launch (start us, length us, event | category | flops | bytes accessed | tf_op | source)
XLA Modules:
  0.0 79.7 jit_solution(3815694021071607982)
XLA Ops:
  0.6 0.0 copy-start.9
  0.6 0.0 copy-start.4
  0.7 0.0 copy-start.3
  0.7 0.0 copy-start.7
  0.7 0.0 copy-start.8
  0.7 0.0 copy-start.2
  0.7 0.0 copy-start.1
  0.7 0.6 copy-done.9
  1.3 0.0 copy-done.7
  1.3 0.0 copy-done.8
  1.4 0.2 select_reduce_fusion.1
  1.6 0.1 select_divide_fusion
  1.6 0.0 copy-done.4
  1.6 0.1 copy.28
  1.7 0.0 copy-done.3
  1.7 0.1 copy.29
  1.8 0.7 fusion.7.fac
  2.5 0.8 div.21.row_weight
  3.3 0.0 copy-done.2
  3.3 0.0 copy-done.1
  3.3 0.7 pad_maximum_fusion.tok
  4.0 71.9 %shard_map.147 = (bf16[16,8192]{1,0:T(8,128)(2,1)}, bf16[16,64]{1,0:T(8,128)(2,1)}, bf16[16,64]{1,0:T(8,128)(2,1)}, bf16[16,8192]{1,0:T(8,128)(2,1)}) custom-call(bf16[16,8192]{1,0:T(8,128)(2,1)} %pad_maximum_fusion.tok, bf16[64,8192]{1,0:T(8,128)(2,1)} %bitcast.18, bf16[16,8192]{1,0:T(8,128)(2,1)} %bitcast.20, bf16[64,8192]{1,0:T(8,128)(2,1)} %bitcast.19, ...), custom_call_target="tpu_custom_call" | custom-call | tf_op jit(solution)/shard_map/pallas_call | solution.py:920
  76.0 0.0 copy-start.6
  76.0 0.0 copy-start
  76.0 1.7 %copy.40 = bf16[1,1,16,8192]{3,2,1,0:T(8,128)(2,1)} copy(bf16[1,1,16,8192]{3,2,1,0:T(8,128)(2,1)} %bitcast.23) | data formatting | bytes 524288
  77.7 0.0 copy-done.6
  77.7 0.0 copy-start.5
  77.7 0.6 copy.41
  78.3 0.1 copy-done.5
  78.4 0.6 copy.42
  79.0 0.0 copy-done
  79.0 0.7 copy.43
  (2 shorter events, 0.0 us)
Async XLA Ops:
  0.6 0.7 copy-start.9
  0.6 1.0 %copy-start.4 = (bf16[1,1,16,64]{3,2,1,0:T(8,128)(2,1)S(1)}, bf16[1,1,16,64]{3,2,1,0:T(8,128)(2,1)}, u32[]{:S(2)}) copy-start(bf16[1,1,16,64]{3,2,1,0:T(8,128)(2,1)} %param.18) | copy-start | bytes 6148
  0.7 1.1 %copy-start.3 = (bf16[1,1,16,64]{3,2,1,0:T(8,128)(2,1)S(1)}, bf16[1,1,16,64]{3,2,1,0:T(8,128)(2,1)}, u32[]{:S(2)}) copy-start(bf16[1,1,16,64]{3,2,1,0:T(8,128)(2,1)} %param.19) | copy-start | bytes 6148
  0.7 0.7 copy-start.7
  0.7 0.7 copy-start.8
  0.7 2.6 %copy-start.2 = (bf16[1,8,8192]{2,1,0:T(8,128)(2,1)S(1)}, bf16[1,8,8192]{2,1,0:T(8,128)(2,1)}, u32[]{:S(2)}) copy-start(bf16[1,8,8192]{2,1,0:T(8,128)(2,1)} %param.12) | copy-start | bytes 393220
  0.7 2.6 %copy-start.1 = (bf16[1,8,8192]{2,1,0:T(8,128)(2,1)S(1)}, bf16[1,8,8192]{2,1,0:T(8,128)(2,1)}, u32[]{:S(2)}) copy-start(bf16[1,8,8192]{2,1,0:T(8,128)(2,1)} %param.13) | copy-start | bytes 393220
  76.0 1.7 %copy-start.6 = (bf16[16,64]{1,0:T(8,128)(2,1)S(1)}, bf16[16,64]{1,0:T(8,128)(2,1)}, u32[]{:S(2)}) copy-start(bf16[16,64]{1,0:T(8,128)(2,1)} %get-tuple-element.9) | copy-start | bytes 6148
  76.0 3.0 %copy-start = (bf16[16,8192]{1,0:T(8,128)(2,1)S(1)}, bf16[16,8192]{1,0:T(8,128)(2,1)}, u32[]{:S(2)}) copy-start(bf16[16,8192]{1,0:T(8,128)(2,1)} %get-tuple-element.11) | copy-start | bytes 786436
  77.7 0.7 copy-start.5
